TPU v7x, 128 devices: a whole 4x4x4 slice. The times are simulated.
128 devices in a mesh: seq: 16 (over y, x_hi, core), batch: 4 (over z), mp: 2 (over x_lo).
Axes of the slice: x: 4 (x_hi: 2, x_lo: 2; x = x_hi * 2 + x_lo), y: 4, z: 4, core: 2. Of those that a mesh axis runs over, the one named last changes fastest.
Arguments:
- hidden: bfloat16 [24576, 7168], P(('seq', 'batch'), 'mp'), may hold values from -192 to 192
- kv_down: bfloat16 [7168, 576], P('mp', 'batch'), may hold values from -0.0625 to 0.0625
- kv_gain: float32 [512], replicated, may hold values from 0.1 to 1.9
- page_owner: int32 [1536, 1], P(('seq', 'batch')), may hold values from 0 to 3; in each aligned block of 24 rows (0 to 23, 24 to 47, ...) at most 12 rows name the same one
- page_request: int32 [1536], P(('seq', 'batch')), may hold values from 0 to 7
- queries: bfloat16 [4, 32, 128, 576], P(None, 'batch', 'mp'), may hold values from -6 to 6
- cache: bfloat16 [32, 8192, 576], P('batch', 'seq'), may hold values from -6 to 6
- lengths: int32 [32], P('batch'), may hold values from 1 to 8192
Outputs:
- attended: float32 [4, 32, 128, 512], P(None, 'batch', 'mp', 'seq')
Inputs may be any that keep to these rules, and one draw needn't show every extreme that they name: `page_owner`: among the pages of one device, at most 12 share an owner.
All inputs are finite; a program needn't handle non-finite values.
Results may differ from a plain program's by a relative error of at most 0.0022.
Values may be sent and summed in bfloat16 or wider, within the bound.
A program may use at most 128 MiB of HBM per device.

v0:
```python
import jax
import jax.numpy as jnp
from jax import lax
from jax.sharding import PartitionSpec as P

eps_norm = 1e-06
score_scale = 192.0 ** (-0.5)
rope_base = 10000.0
masked_value = -1e30


def finish_rows(portion, squares, gain, latent_width, rope_width, positions):
    breadth = portion.shape[1]
    columns = jnp.arange(breadth)
    inverse = lax.rsqrt(squares / latent_width + eps_norm)[:, None]
    gain_full = jnp.concatenate([gain, jnp.ones((rope_width,), gain.dtype)])
    normed = portion * inverse * gain_full[None, :]
    half_rope = rope_width // 2
    offsets = columns - latent_width
    pair_index = jnp.where(offsets >= 0, offsets % half_rope, 0)
    frequency = rope_base ** (-pair_index.astype(portion.dtype) / half_rope)
    angles = positions[:, None] * frequency[None, :]
    ahead = jnp.roll(portion, -half_rope, axis=1)
    behind = jnp.roll(portion, half_rope, axis=1)
    cosine = jnp.cos(angles)
    sine = jnp.sin(angles)
    rotated = jnp.where(
        (offsets < half_rope)[None, :],
        portion * cosine - ahead * sine,
        portion * cosine + behind * sine,
    )
    return jnp.where((columns >= latent_width)[None, :], rotated, normed).astype(jnp.bfloat16)


def on_device(hidden, kv_down, kv_gain, page_owner, page_request, queries, cache, lengths):
    token_count = hidden.shape[0]
    page_count = page_request.shape[0]
    page_length = token_count // page_count
    latent_width = kv_gain.shape[0]
    kv_width = queries.shape[3]
    rope_width = kv_width - latent_width
    owner_count = lax.axis_size("batch")
    capacity = max(2, 2 * page_count // owner_count)
    positions = jnp.arange(token_count).astype(jnp.float32)
    partial_sum = jnp.dot(
        hidden,
        lax.all_gather(kv_down, "batch", axis=1, tiled=True),
        preferred_element_type=jnp.float32,
    )
    latent = lax.psum(partial_sum, "mp")
    squares = jnp.sum(latent[:, :latent_width] * latent[:, :latent_width], axis=1)
    rows = finish_rows(latent, squares, kv_gain, latent_width, rope_width, positions)
    row_breadth = rows.shape[1]
    page_rows = rows.reshape(page_count, page_length * row_breadth)
    owners = page_owner[:, 0]
    marked = (owners[:, None] == jnp.arange(owner_count)[None, :]).astype(jnp.int32)
    earlier = jnp.cumsum(marked, axis=0) - marked
    ranking = jnp.sum(earlier * marked, axis=1)
    destination = owners * capacity + ranking
    select = (destination[None, :] == jnp.arange(owner_count * capacity)[:, None]).astype(
        jnp.bfloat16
    )
    packed = jnp.dot(select, page_rows, preferred_element_type=jnp.float32).astype(jnp.bfloat16)
    packed = packed.reshape(owner_count, capacity, page_length * row_breadth)
    labels = jnp.dot(
        select, (page_request + 1).astype(jnp.bfloat16)[:, None], preferred_element_type=jnp.float32
    )
    labels = labels.astype(jnp.bfloat16).reshape(owner_count, capacity)
    arrived, arrived_labels = (
        lax.all_to_all(packed, "batch", split_axis=0, concat_axis=0, tiled=True),
        lax.all_to_all(labels, "batch", split_axis=0, concat_axis=0, tiled=True),
    )
    arrived = arrived.reshape(owner_count, capacity, page_length, row_breadth)
    moved = arrived.reshape(owner_count * capacity * page_length, kv_width)
    token_labels = jnp.repeat(arrived_labels.reshape(-1).astype(jnp.int32), page_length)
    request_count = cache.shape[0]
    context = cache.shape[1]
    cache_positions = lax.axis_index("seq") * context + jnp.arange(context)
    live_resident = cache_positions[None, :] < lengths[:, None]
    live_moved = token_labels[None, :] == (jnp.arange(request_count) + 1)[:, None]
    resident_scores = (
        jnp.einsum("srhk,rtk->srht", queries, cache, preferred_element_type=jnp.float32)
        * score_scale
    )
    moved_scores = (
        jnp.einsum("srhk,tk->srht", queries, moved, preferred_element_type=jnp.float32)
        * score_scale
    )
    scores = jnp.concatenate([resident_scores, moved_scores], axis=3)
    live = jnp.concatenate([live_resident, live_moved], axis=1)[None, :, None, :]
    masked = jnp.where(live, scores, masked_value)
    local_peak = jnp.max(masked, axis=3)
    highest = lax.pmax(local_peak, "seq")
    weights = jnp.where(live, jnp.exp(masked - highest[..., None]), 0.0)
    totals = jnp.sum(weights, axis=3)
    rounded = weights.astype(jnp.bfloat16)
    numerator = jnp.einsum(
        "srht,rtl->srhl",
        rounded[..., :context],
        cache[..., :latent_width],
        preferred_element_type=jnp.float32,
    )
    numerator = numerator + jnp.einsum(
        "srht,tl->srhl",
        rounded[..., context:],
        moved[:, :latent_width],
        preferred_element_type=jnp.float32,
    )
    whole_total, whole_numer = lax.psum((totals, numerator), "seq")
    column_count = latent_width // lax.axis_size("seq")
    mine = lax.dynamic_slice_in_dim(
        whole_numer, lax.axis_index("seq") * column_count, column_count, 3
    )
    attended = mine / whole_total[..., None]
    return attended


def solution(mesh):
    return jax.shard_map(
        on_device,
        mesh=mesh,
        in_specs=(
            P(("seq", "batch"), "mp"),
            P("mp", "batch"),
            P(),
            P(("seq", "batch"), None),
            P(("seq", "batch")),
            P(None, "batch", "mp", None),
            P("batch", "seq", None),
            P("batch"),
        ),
        out_specs=P(None, "batch", "mp", "seq"),
        check_vma=False,
    )
```

profile of v0, /device:TPU:1, one launch (start us, length us, event | category | flops | bytes accessed | tf_op | source)
XLA Modules:
  0.0 398.5 jit_solution(5570476112090676473)
XLA Ops:
  11.1 5.9 %all-to-all-start = ((bf16[4,1,12]{2,1,0:T(2,128)(2,1)}), bf16[4,1,12]{2,1,0:T(2,128)(2,1)S(1)}, u32[]{:S(2)}, u32[]{:S(2)}) async-start(bf16[4,1,12]{2,1,0:T(2,128)(2,1)} %all_to_all.12), calls=%async_computation | async-start | bytes 4096 | tf_op jit(solution)/shard_map/all_to_all | solution.py:71
  17.7 42.5 %all-gather.2.cloned.1.call-done = bf16[3584,576]{0,1:T(8,128)(2,1)} async-done(((bf16[3584,144]{0,1:T(8,128)(2,1)}), bf16[3584,576]{0,1:T(8,128)(2,1)}) %all-gather.2.cloned.1.call-update) | async-done | bytes 4128784 | tf_op jit(solution)/shard_map/all_gather | solution.py:47
  60.2 5.4 %fusion.48 = f32[384,576]{0,1:T(8,128)} fusion(bf16[384,3584]{1,0:T(8,128)(2,1)S(1)} %copy-done, bf16[3584,576]{0,1:T(8,128)(2,1)} %all-gather.2.cloned.1.call-done), kind=kOutput, calls=%fused_computation.72 | convolution fusion | flops 1585446912 | bytes 7766016 | tf_op jit(solution)/shard_map/dot_general | solution.py:45
  65.7 7.0 %multiply_bitcast_fusion.1 = f32[4,8,64,512]{3,2,0,1:T(8,128)} fusion(bf16[4,8,64,576]{3,2,1,0:T(8,128)(2,1)} %param.13, bf16[8,512,576]{1,2,0:T(8,128)(2,1)} %param.14), kind=kOutput, calls=%fused_computation.13 | convolution fusion | flops 1209008128 | bytes 11272192 | tf_op jit(solution)/shard_map/srhk,rtk->srht/dot_general | solution.py:82
  72.7 36.3 %all-reduce.4.cloned.1.call-done = f32[384,576]{0,1:T(8,128)} async-done(((f32[384,576]{0,1:T(8,128)}), f32[384,576]{0,1:T(8,128)}) %all-reduce.4.cloned.1.call-update) | async-done | bytes 884752 | tf_op jit(solution)/shard_map/psum | solution.py:50
  109.0 1.3 fusion.28
  111.2 1.5 fusion.47
  112.7 5.2 %fusion.25 = bf16[384,576]{0,1:T(8,128)(2,1)} fusion(f32[384,576]{0,1:T(8,128)S(1)} %copy-done.3, f32[384,32]{0,1:T(8,128)S(1)} %get-tuple-element.8, f32[384,544]{0,1:T(8,128)S(1)} %get-tuple-element.10, f32[384,544]{0,1:T(8,128)S(1)} %get-tuple-element.9, f32[384,32]{0,1:T(8,128)S(1)} %get-tuple-element.7, f32[576]{0:T(1024)S(1)} %concatenate.20, ...), kind=kLoop, calls=%fused_computation.29 | loop fusion | flops 2875392 | bytes 3105408 | tf_op jit(solution)/shard_map/convert_element_type | solution.py:32
  117.8 1.3 copy.26
  120.3 2.4 convolution_convert_fusion
  122.6 2.4 reshape.79
  125.0 4.3 %all-to-all-start.1 = ((bf16[4,12,9216]{2,1,0:T(8,128)(2,1)}), bf16[4,12,9216]{2,1,0:T(8,128)(2,1)}, u32[]{:S(2)}, u32[]{:S(2)}) async-start(bf16[4,12,9216]{2,1,0:T(8,128)(2,1)} %reshape.79), calls=%async_computation.1 | async-start | bytes 2359296 | tf_op jit(solution)/shard_map/all_to_all | solution.py:70
  129.7 15.3 %all-to-all-done.1 = bf16[4,12,9216]{2,1,0:T(8,128)(2,1)} async-done(((bf16[4,12,9216]{2,1,0:T(8,128)(2,1)}), bf16[4,12,9216]{2,1,0:T(8,128)(2,1)}, u32[]{:S(2)}, u32[]{:S(2)}) %all-to-all-start.1) | async-done | bytes 884768 | tf_op jit(solution)/shard_map/all_to_all | solution.py:70
  145.1 2.8 reshape_reshape.3
  147.8 4.9 %multiply_bitcast_fusion = f32[4,8,64,768]{3,2,1,0:T(8,128)S(1)} fusion(bf16[4,8,64,576]{3,2,1,0:T(8,128)(2,1)} %param.13, bf16[768,576]{1,0:T(8,128)(2,1)} %reshape_reshape.3), kind=kOutput, calls=%fused_computation.5 | convolution fusion | flops 1813512192 | bytes 9535488 | tf_op jit(solution)/shard_map/srhk,tk->srht/dot_general | solution.py:86
  152.7 2.7 copy-done.1
  156.6 63.9 %pmax.7 = f32[4,8,64]{2,1,0:T(8,128)S(1)} all-reduce(f32[4,8,64]{2,1,0:T(8,128)S(1)} %fusion.2), channel_id=1, replica_groups=mesh['seq'=16,'batch'=4,'mp'=2] {'seq'}, use_global_device_ids=true, to_apply=%region_5.6 | all-reduce | flops 2048 | bytes 16384 | tf_op jit(solution)/shard_map/pmax | solution.py:93
  220.5 6.4 %fusion = (f32[4,8,64]{2,1,0:T(8,128)S(1)}, bf16[4,8,64,1280]{3,2,1,0:T(8,128)(2,1)S(1)}) fusion(f32[4,8,64,768]{3,2,1,0:T(8,128)} %copy-done.1, f32[4,8,64]{2,1,0:T(8,128)S(1)} %pmax.7, pred[8,1280]{1,0:T(8,128)(4,1)S(1)} %pad_add_fusion, f32[4,8,64,512]{3,2,0,1:T(8,128)} %multiply_bitcast_fusion.1), kind=kLoop, calls=%fused_computation.3 | loop fusion | flops 15726592 | bytes 15755264 | tf_op jit(solution)/shard_map/reduce_sum | solution.py:95
  226.9 1.8 fusion.8
  228.7 3.3 bitcast_add_fusion
  232.0 65.0 %psum.23 = f32[4,8,64]{2,1,0:T(8,128)S(1)} all-reduce(f32[4,8,64]{2,1,0:T(8,128)S(1)} %get-tuple-element.5), channel_id=1, replica_groups=mesh['seq'=16,'batch'=4,'mp'=2] {'seq'}, use_global_device_ids=true, to_apply=%region_8.9 | all-reduce | flops 2048 | bytes 16384 | tf_op jit(solution)/shard_map/psum | solution.py:109
  297.1 89.7 %all-reduce.6.cloned.1.call-done = f32[4,8,64,512]{3,2,0,1:T(8,128)} async-done(((f32[4,8,64,512]{3,2,0,1:T(8,128)}), f32[4,8,64,512]{3,2,0,1:T(8,128)}) %all-reduce.6.cloned.1.call-update) | async-done | bytes 4194320 | tf_op jit(solution)/shard_map/psum | solution.py:109
  386.8 2.8 dynamic-slice_divide_fusion
  389.6 2.3 copy.34
  (47 shorter events, 9.0 us)
Async XLA Ops:
  6.5 53.7 %copy-start = (bf16[384,3584]{1,0:T(8,128)(2,1)S(1)}, bf16[384,3584]{1,0:T(8,128)(2,1)}, u32[]{:S(2)}) copy-start(bf16[384,3584]{1,0:T(8,128)(2,1)} %param.8) | copy-start | bytes 8257540
  6.5 53.7 %all-gather.2.cloned.1.call-start = ((), (), s32[]{:S(2)}) async-start(), calls=%async_computation.2 | async-start | bytes 5160960 | tf_op jit(solution)/shard_map/all_gather | solution.py:47
  11.1 113.9 %all-to-all-start = ((bf16[4,1,12]{2,1,0:T(2,128)(2,1)}), bf16[4,1,12]{2,1,0:T(2,128)(2,1)S(1)}, u32[]{:S(2)}, u32[]{:S(2)}) async-start(bf16[4,1,12]{2,1,0:T(2,128)(2,1)} %all_to_all.12), calls=%async_computation | async-start | bytes 4096 | tf_op jit(solution)/shard_map/all_to_all | solution.py:71
  17.0 92.0 %all-reduce.4.cloned.1.call-start = ((), (), s32[]{:S(2)}) async-start(), calls=%async_computation.3 | async-start | bytes 1769472 | tf_op jit(solution)/shard_map/psum | solution.py:50
  17.7 48.0 %copy-start.5 = (s32[8]{0:T(128)S(1)}, s32[8]{0:T(128)}, u32[]{:S(2)}) copy-start(s32[8]{0:T(128)} %param.15) | copy-start | bytes 100
  109.0 3.7 copy-start.3
  125.0 20.0 %all-to-all-start.1 = ((bf16[4,12,9216]{2,1,0:T(8,128)(2,1)}), bf16[4,12,9216]{2,1,0:T(8,128)(2,1)}, u32[]{:S(2)}, u32[]{:S(2)}) async-start(bf16[4,12,9216]{2,1,0:T(8,128)(2,1)} %reshape.79), calls=%async_computation.1 | async-start | bytes 2359296 | tf_op jit(solution)/shard_map/all_to_all | solution.py:70
  129.3 257.5 %all-reduce.6.cloned.1.call-start = ((), (), s32[]{:S(2)}) async-start(), calls=%async_computation.4 | async-start | bytes 8388608 | tf_op jit(solution)/shard_map/psum | solution.py:109
  147.8 7.6 %copy-start.2 = (f32[4,8,64,512]{3,2,0,1:T(8,128)S(1)}, f32[4,8,64,512]{3,2,0,1:T(8,128)}, u32[]{:S(2)}) copy-start(f32[4,8,64,512]{3,2,0,1:T(8,128)} %multiply_bitcast_fusion.1) | copy-start | bytes 12582916
  152.7 2.7 copy-start.1
  220.5 6.4 %copy-start.4 = (bf16[768,576]{1,0:T(8,128)(2,1)S(1)}, bf16[768,576]{1,0:T(8,128)(2,1)}, u32[]{:S(2)}) copy-start(bf16[768,576]{1,0:T(8,128)(2,1)} %reshape_reshape.3) | copy-start | bytes 2654212
  220.5 8.2 %slice-start = ((s8[4718592]{0:T(1024)(128)(4,1)}), s8[4194304]{0:T(1024)(128)(4,1)S(1)}, s32[]{:S(2)}) async-start(s8[4718592]{0:T(1024)(128)(4,1)} %bitcast.41), calls=%async_computation.5 | async-start | bytes 8388608
  226.9 1.8 slice-start.1
Sparse Core Ops, SparseCore 0:
  9.0 51.1 all-gather.1
  65.8 43.1 all-reduce.3
  232.1 154.6 all-reduce.5
where the time goes:
time: 401 us; the launch traced here: 398 us
  waiting for transfers between devices  185 us (46%)
  blocking collectives  129 us (32%)
  matrix products  25.5 us (6%)
  other arithmetic  19.5 us (5%)
  local copies, waits for them, and re-layouts  16.6 us (4%)
  between operations  13.2 us (3%)
  starting transfers between devices  10.2 us (3%)
    psum x1, waiting for transfers between devices, on_device(): whole_total, whole_numer = lax.psum((totals, numerator), 'seq')  89.7 us
    psum x1, blocking collectives, on_device(): whole_total, whole_numer = lax.psum((totals, numerator), 'seq')  65 us
    pmax x1, blocking collectives, on_device(): highest = lax.pmax(local_peak, 'seq')  63.9 us
    all_gather x1, waiting for transfers between devices, on_device(): lax.all_gather(kv_down, 'batch', axis=1, tiled=True)  42.5 us
    psum x1, waiting for transfers between devices, on_device(): latent = lax.psum(partial_sum, 'mp')  36.3 us
    all_to_all x1, waiting for transfers between devices, on_device(): lax.all_to_all(packed, 'batch', split_axis=0, concat_axis=0, tiled=True)  15.3 us
  transfers between devices with their start and end apart: 5, of which 4 were waited for; matrix products, arithmetic and copies ran while one was open for 8% of the time, Pallas kernels for 0%

commit v1 on v0

v1 whole, which is shorter than its diff:
```python
import jax
import jax.numpy as jnp
import numpy as np
from jax import lax
from jax.experimental import pallas as pl
from jax.experimental.pallas import tpu as pltpu
from jax.sharding import PartitionSpec as P

MESH = pl.DeviceIdType.MESH
F32, BF16, I32, I16 = jnp.float32, jnp.bfloat16, jnp.int32, jnp.int16

eps_norm = 1e-06
score_scale = 192.0 ** (-0.5)
log2_scale = score_scale * 1.4426950408889634
rope_base = 10000.0
masked_value = -1e30
floor_value = -1e29
code_top = 32767.0

TOK, HALF_D, KVW, LATW, ROPEW = 384, 3584, 576, 512, 64
LABELS = 64
KVX = KVW + LABELS
BLK = 144
SHARE, DIRECT = 256, 384
CAPTOK = 192
PAGES, PAGE, CAP = 24, 16, 12
QROWS = 256
CTXD = 512
NR = 4


def nt(a, b):
    return lax.dot_general(a, b, (((1,), (1,)), ((), ())), preferred_element_type=F32)


def nn(a, b):
    return jnp.dot(a, b, preferred_element_type=F32)


def kernel(
    hidden, kv_down, gain, owner, request, queries, cache, lengths, cosine, sine,
    out,
    hid, kvt, lat, mps, mpr, mss, msr, rows, packed, relay, arr, tok,
    qraw, qbuf, kbuf, acc, ms, ls, osend, ostat, ybuf, ystat, rsend, rstat, mbuf, mstat, xbuf, xstat, fin,
    loc, send, recv,
):
    s, b, p = lax.axis_index("seq"), lax.axis_index("batch"), lax.axis_index("mp")
    c = lax.rem(s, 2)
    sib = s + 1 - 2 * c
    y = lax.div(s, 4)
    in_y = lax.rem(s, 4)
    xh = lax.rem(lax.div(s, 2), 2)
    dev_zp = (s, lax.rem(b + 1, 4), p)
    dev_zm = (s, lax.rem(b + 3, 4), p)
    dev_zz = (s, lax.rem(b + 2, 4), p)
    dev_mp = (s, b, 1 - p)
    dev_sib = (sib, b, p)
    dev_yp = (lax.rem(y + 1, 4) * 4 + in_y, b, p)
    dev_ym = (lax.rem(y + 3, 4) * 4 + in_y, b, p)
    dev_x = (s + 2 - 4 * xh, b, p)

    used = [0]
    started = []

    def link(src, dst, dev):
        i = used[0]
        used[0] += 1
        return pltpu.make_async_remote_copy(
            src_ref=src, dst_ref=dst, send_sem=send.at[i], recv_sem=recv.at[i],
            device_id=dev, device_id_type=MESH,
        )

    def go(copy):
        copy.start()
        started.append(copy)

    def code(value, axis):
        most = jnp.max(jnp.abs(value), axis=axis, keepdims=True)
        return jnp.round(value * (code_top / jnp.maximum(most, 1e-30))), most * (1.0 / code_top)

    def to_code(value):
        return value.astype(I32).astype(I16)

    def from_code(coded):
        return coded.astype(I32).astype(F32)

    def go_pair(pair):
        go(pair[0])
        go(pair[1])

    def wait_pair(pair):
        pair[0].wait_recv()
        pair[1].wait_recv()

    load_kv = pltpu.make_async_copy(kv_down, kvt.at[0], loc.at[0])
    load_kv.start()
    load_hid = pltpu.make_async_copy(hidden, hid, loc.at[1])
    load_hid.start()
    load_q = []
    for step in range(4):
        load_q.append(pltpu.make_async_copy(queries.at[step, pl.ds(c * NR, NR)], qraw.at[:, step], loc.at[2 + step]))
        load_q[-1].start()
    load_cache = pltpu.make_async_copy(cache.at[pl.ds(c * NR, NR)], kbuf.at[0], loc.at[6])
    load_cache.start()

    barrier = pltpu.get_barrier_semaphore()
    for dev in (dev_zp, dev_zm, dev_zz, dev_mp, dev_sib, dev_yp, dev_ym, dev_x):
        pl.semaphore_signal(barrier, inc=1, device_id=dev, device_id_type=MESH)

    load_kv.wait()
    pl.semaphore_wait(barrier, 8)

    base = c * (HALF_D // 2)

    def lanes(start, size):
        return pl.ds(pl.multiple_of(base + start, 128), size)

    def kv_link(slot, to_slot, at, dev):
        return link(kvt.at[slot, :, at], kvt.at[to_slot, :, at], dev)

    def part_of(k, first=0, size=SHARE):
        return lanes(lax.rem(y + k, 4) * SHARE + first, size)

    low, high = lanes(4 * SHARE, DIRECT), lanes(4 * SHARE + DIRECT, DIRECT)
    mine = part_of(0)
    s_p, s_m = kv_link(0, 1, mine, dev_zp), kv_link(0, 2, mine, dev_zm)
    d_p0, d_m1 = kv_link(0, 1, low, dev_zp), kv_link(0, 2, high, dev_zm)
    d_p1, d_m0 = kv_link(0, 1, high, dev_zp), kv_link(0, 2, low, dev_zm)
    for copy in (s_p, s_m, d_p0, d_m1, d_p1, d_m0):
        go(copy)
    cache_out = link(cache.at[pl.ds((1 - c) * NR, NR)], kbuf.at[1], dev_sib)
    go(cache_out)
    sf_p, sf_m = (
        kv_link(1, 3, part_of(0, 0, SHARE // 2), dev_zp),
        kv_link(2, 3, part_of(0, SHARE // 2, SHARE // 2), dev_zm),
    )
    df_p, df_m = kv_link(1, 3, low, dev_zp), kv_link(2, 3, high, dev_zm)
    near_p = [None] + [kv_link(slot, slot, mine, dev_yp) for slot in (1, 2, 3)]
    near_m = [None] + [kv_link(slot, slot, mine, dev_ym) for slot in (1, 2, 3)]
    far = [
        None,
        [kv_link(1, 1, part_of(3), dev_yp)],
        [kv_link(2, 2, part_of(1), dev_ym)],
        [
            kv_link(3, 3, part_of(3, 0, SHARE // 2), dev_yp),
            kv_link(3, 3, part_of(1, SHARE // 2, SHARE // 2), dev_ym),
        ],
    ]
    share_s = [None] + [kv_link(slot, slot, lanes(0, 4 * SHARE), dev_sib) for slot in (1, 2, 3)]
    share_d = [None] + [kv_link(slot, slot, lanes(4 * SHARE, 2 * DIRECT), dev_sib) for slot in (1, 2, 3)]

    token = lax.broadcasted_iota(I32, (1, TOK), 1)
    token_page = lax.shift_right_logical(token, 4)
    dest = jnp.zeros((1, TOK), I32)
    asked = jnp.zeros((1, TOK), I32)
    counts = [jnp.int32(0)] * 4
    for page in range(PAGES):
        to = owner[0, page]
        rank = jnp.where(to == 0, counts[0], jnp.where(to == 1, counts[1], jnp.where(to == 2, counts[2], counts[3])))
        counts = [counts[o] + (to == o).astype(I32) for o in range(4)]
        dest = jnp.where(token_page == page, (to * CAP + rank) * PAGE, dest)
        asked = jnp.where(token_page == page, request[page] + 1, asked)
    dest = dest + lax.bitwise_and(token, 15)
    tok[...] = dest

    label_row = lax.broadcasted_iota(I32, (LABELS, TOK), 0)
    rows[KVW:, :] = (label_row == asked).astype(F32).astype(BF16)

    origin = [lax.rem(b + ahead, 4) for ahead in (0, 3, 1, 2)]
    m_copies = [
        (link(mps.at[slot], mpr.at[slot], dev_mp), link(mss.at[slot], msr.at[slot], dev_mp)) for slot in range(3)
    ]
    tails = (slice(0, 256), slice(256, TOK))
    for at in tails:
        at = pl.ds(at.start, at.stop - at.start)
        m_copies.append((
            link(mps.at[3, :, at], mpr.at[3, :, at], dev_mp), link(mss.at[3, :, at], msr.at[3, :, at], dev_mp),
        ))

    def send_part(slot, part, copies, at=slice(None)):
        lat[origin[slot], :, at] = part
        coded, scale = code(part, 0)
        mps[slot, :, at] = to_code(coded)
        mss[slot, :, at] = scale
        go_pair(copies)

    def weigh(score, top):
        return jnp.exp2(score * log2_scale - top * log2_scale)

    def fold(w):
        total = w[:, :128]
        for j in range(1, w.shape[1] // 128):
            total = total + w[:, j * 128:j * 128 + 128]
        return total

    def peak(score):
        most = score[:, :128]
        for j in range(1, score.shape[1] // 128):
            most = jnp.maximum(most, score[:, j * 128:j * 128 + 128])
        return most

    def resident(r, carry):
        q = qbuf[r, :, :KVW]
        length = lengths[c * NR + r]
        at = lax.broadcasted_iota(I32, (1, CTXD), 1)
        score0 = jnp.where(at + s * CTXD < length, nn(q, kbuf[0, r]), masked_value)
        score1 = jnp.where(at + sib * CTXD < length, nn(q, kbuf[1, r]), masked_value)
        top = jnp.max(jnp.maximum(peak(score0), peak(score1)), axis=1, keepdims=True)
        top = jnp.maximum(top, floor_value)
        w0 = weigh(score0, top)
        w1 = weigh(score1, top)
        acc[r] = nt(w0.astype(BF16), kbuf[0, r, :LATW, :]) + nt(w1.astype(BF16), kbuf[1, r, :LATW, :])
        ms[r] = jnp.broadcast_to(top, (QROWS, 128))
        ls[r] = fold(w0) + fold(w1)
        return carry

    load_hid.wait()
    s_p.wait_recv()
    go(sf_p)
    go(near_p[1])
    go(near_m[1])
    s_m.wait_recv()
    go(sf_m)
    go(near_p[2])
    go(near_m[2])
    send_part(0, nt(kvt[0], hid[...]), m_copies[0])

    near_p[1].wait_recv()
    go(far[1][0])
    near_m[2].wait_recv()
    go(far[2][0])
    d_p0.wait_recv()
    go(df_p)
    d_m1.wait_recv()
    go(df_m)
    sf_p.wait_recv()
    sf_m.wait_recv()
    go(near_p[3])
    go(near_m[3])

    for copy in load_q:
        copy.wait()
    load_cache.wait()
    cache_out.wait_recv()
    label_at = lax.broadcasted_iota(I32, (QROWS, LABELS), 1)
    for r in range(NR):
        qbuf[r, :, :KVW] = qraw[r].reshape(QROWS, KVW)
        qbuf[r, :, KVW:] = jnp.where(label_at == c * NR + r + 1, 0.0, masked_value).astype(BF16)
    lax.fori_loop(0, 1, resident, 0)

    d_p1.wait_recv()
    go(share_d[1])
    d_m0.wait_recv()
    go(share_d[2])
    near_m[1].wait_recv()
    far[1][0].wait_recv()
    go(share_s[1])
    near_p[2].wait_recv()
    far[2][0].wait_recv()
    go(share_s[2])
    near_p[3].wait_recv()
    go(far[3][0])
    near_m[3].wait_recv()
    go(far[3][1])
    lax.fori_loop(1, 2, resident, 0)

    df_p.wait_recv()
    df_m.wait_recv()
    go(share_d[3])
    for slot in (1, 2):
        share_d[slot].wait_recv()
        share_s[slot].wait_recv()
    both = nt(kvt[1:3].reshape(2 * BLK, HALF_D), hid[...])
    for slot in (1, 2):
        send_part(slot, both[(slot - 1) * BLK:slot * BLK], m_copies[slot])

    far[3][0].wait_recv()
    far[3][1].wait_recv()
    go(share_s[3])
    share_d[3].wait_recv()
    share_s[3].wait_recv()
    for i, at in enumerate(tails):
        send_part(3, nt(kvt[3], hid[at, :]), m_copies[3 + i], at)

    for slot in range(4):
        for pair in m_copies[slot:] if slot == 3 else m_copies[slot:slot + 1]:
            wait_pair(pair)
        lat[origin[slot]] = lat[origin[slot]] + from_code(mpr[slot]) * msr[slot]
    whole = lat[...].reshape(KVW, TOK)
    latent = whole[:LATW]
    inverse = lax.rsqrt(jnp.sum(latent * latent, axis=0, keepdims=True) / LATW + eps_norm)
    gain_cols = jnp.transpose(jnp.broadcast_to(gain[...], (128, LATW)))
    for j in range(TOK // 128):
        at = slice(j * 128, j * 128 + 128)
        rows[:LATW, at] = (latent[:, at] * inverse[:, at] * gain_cols).astype(BF16)
    first, second = whole[LATW:LATW + ROPEW // 2], whole[LATW + ROPEW // 2:]
    rows[LATW:LATW + ROPEW // 2, :] = (first * cosine[...] - second * sine[...]).astype(BF16)
    rows[LATW + ROPEW // 2:KVW, :] = (first * sine[...] + second * cosine[...]).astype(BF16)

    slot_at = lax.broadcasted_iota(I32, (CAPTOK, TOK), 0)

    def pack_for(to):
        chosen = ((slot_at + to * CAPTOK) == tok[...]).astype(F32)
        empty = jnp.sum(chosen, axis=1, keepdims=True) < 0.5
        page_rows = nt(chosen.astype(BF16), rows[...])
        column = lax.broadcasted_iota(I32, (CAPTOK, KVX), 1)
        return jnp.where((column == KVW) & empty, 1.0, page_rows).astype(BF16)

    half = CAPTOK // 2
    a_r0 = link(packed.at[2, pl.ds(0, half)], relay.at[0], dev_zp)
    a_r1 = link(packed.at[2, pl.ds(half, half)], relay.at[1], dev_zm)
    a_p = link(packed.at[0], arr.at[1, c], dev_zp)
    a_m = link(packed.at[1], arr.at[2, c], dev_zm)
    a_f0 = link(relay.at[0], arr.at[3, c, pl.ds(0, half)], dev_zp)
    a_f1 = link(relay.at[1], arr.at[3, c, pl.ds(half, half)], dev_zm)
    a_share = [link(arr.at[slot, c], arr.at[slot, c], dev_sib) for slot in range(3)]
    a_share3 = [
        link(arr.at[3, c, pl.ds(0, half)], arr.at[3, c, pl.ds(0, half)], dev_sib),
        link(arr.at[3, c, pl.ds(half, half)], arr.at[3, c, pl.ds(half, half)], dev_sib),
    ]
    packed[2] = pack_for(lax.rem(b + 2, 4))
    go(a_r0)
    go(a_r1)
    packed[0] = pack_for(lax.rem(b + 1, 4))
    go(a_p)
    packed[1] = pack_for(lax.rem(b + 3, 4))
    go(a_m)
    arr[0, c] = pack_for(b)
    go(a_share[0])

    def pages_step(r, slots):
        q = qbuf[r]
        old = ms[r][:, :1]
        scores = [nt(q, arr[slot].reshape(2 * CAPTOK, KVX)) for slot in slots]
        most = peak(scores[0])
        for score in scores[1:]:
            most = jnp.maximum(most, peak(score))
        top = jnp.maximum(old, jnp.max(most, axis=1, keepdims=True))
        shrink = jnp.exp2((old - top) * log2_scale)
        total = ls[r] * shrink
        value = acc[r] * shrink
        for slot, score in zip(slots, scores):
            w = weigh(score, top)
            total = total + fold(w)
            value = value + nn(w.astype(BF16), arr[slot].reshape(2 * CAPTOK, KVX)[:, :LATW])
        return value, jnp.broadcast_to(top, (QROWS, 128)), total

    def pages_of(slots):
        def body(r, carry):
            acc[r], ms[r], ls[r] = pages_step(r, slots)
            return carry

        return body

    a_r0.wait_recv()
    go(a_f0)
    a_r1.wait_recv()
    go(a_f1)
    lax.fori_loop(2, NR, resident, 0)
    a_share[0].wait_recv()
    lax.fori_loop(0, NR, pages_of((0,)), 0)
    a_p.wait_recv()
    go(a_share[1])
    a_m.wait_recv()
    go(a_share[2])
    a_share[1].wait_recv()
    a_share[2].wait_recv()
    lax.fori_loop(0, NR, pages_of((1, 2)), 0)
    a_f0.wait_recv()
    go(a_share3[0])
    a_f1.wait_recv()
    go(a_share3[1])
    a_share3[0].wait_recv()
    a_share3[1].wait_recv()

    def merge(parts):
        top = parts[0][1][0]
        for _, stat in parts[1:]:
            top = jnp.maximum(top, stat[0])
        value, total = 0.0, 0.0
        for coded, stat in parts:
            factor = jnp.exp2(stat[0] - top)
            value = value + from_code(coded) * (factor * stat[2])
            total = total + factor * stat[1]
        return value, top, total

    def put(coded_ref, stat_ref, value, top, total):
        coded, scale = code(value, 0)
        coded_ref[...] = to_code(coded)
        stat_ref[0] = top
        stat_ref[1] = total
        stat_ref[2] = scale

    yp, ym, yy = lax.rem(y + 1, 4), lax.rem(y + 3, 4), lax.rem(y + 2, 4)
    y_copies = []
    for r in range(NR):
        pairs = (
            (osend.at[r, yy, 0], ostat.at[r], 0, dev_yp),
            (osend.at[r, yy, 1], ostat.at[r], 1, dev_ym),
            (osend.at[r, yp, 1], ostat.at[r], 2, dev_yp),
            (osend.at[r, ym, 0], ostat.at[r], 3, dev_ym),
            (rsend.at[r, 0], rstat.at[r, 0], 4, dev_yp),
            (rsend.at[r, 1], rstat.at[r, 1], 5, dev_ym),
        )
        y_copies.append([
            (link(data, ybuf.at[r, k], dev), link(stat, ystat.at[r, k], dev)) for data, stat, k, dev in pairs
        ])

    lane = lax.broadcasted_iota(I32, (QROWS, 128), 1)
    for r in range(NR):
        value, top, total = pages_step(r, (3,))
        coded, scale = code(value, 1)
        osend[r] = to_code(jnp.transpose(coded)).reshape(4, 2, 64, QROWS)
        stat = jnp.transpose(jnp.where(lane == 0, top * log2_scale, scale))
        ostat[r, 0] = stat[0:1]
        ostat[r, 1] = jnp.sum(jnp.transpose(total), axis=0, keepdims=True)
        ostat[r, 2] = stat[1:2]
        for k in range(4):
            go_pair(y_copies[r][k])
    for r in range(NR):
        for k, to in ((0, yp), (1, ym)):
            wait_pair(y_copies[r][k])
            put(rsend.at[r, k], rstat.at[r, k], *merge([
                (osend[r, to, k], ostat[r]), (ybuf[r, k], ystat[r, k]),
            ]))
            go_pair(y_copies[r][4 + k])
    x_copies = []
    for r in range(NR):
        for k in range(2, 6):
            wait_pair(y_copies[r][k])
        for h, (one, two) in enumerate(((3, 4), (2, 5))):
            put(mbuf.at[r, h], mstat.at[r, h], *merge([
                (osend[r, y, h], ostat[r]), (ybuf[r, one], ystat[r, one]), (ybuf[r, two], ystat[r, two]),
            ]))
        x_copies.append((
            link(mbuf.at[r, 1 - xh], xbuf.at[r], dev_x), link(mstat.at[r, 1 - xh], xstat.at[r], dev_x),
        ))
        go_pair(x_copies[r])
    c_copies = []
    for r in range(NR):
        wait_pair(x_copies[r])
        value, _, total = merge([(mbuf[r, xh], mstat[r, xh]), (xbuf[r], xstat[r])])
        value = value / total
        for core in range(2):
            for step in range(4):
                fin[r, core, step] = value[32 * core:32 * core + 32, 64 * step:64 * step + 64]
        c_copies.append(link(fin.at[r, 1 - c], out.at[:, c * NR + r], dev_sib))
        go(c_copies[r])
        out[:, c * NR + r] = fin[r, c]
    for copy in c_copies:
        copy.wait_recv()
    for copy in started:
        copy.wait_send()


LINKS = 136


def tables():
    half = ROPEW // 2
    frequency = rope_base ** (-np.arange(half, dtype=np.float32) / np.float32(half))
    angles = np.arange(TOK, dtype=np.float32)[None, :] * frequency.astype(np.float32)[:, None]
    return np.cos(angles).astype(np.float32), np.sin(angles).astype(np.float32)


def on_device(hidden, kv_down, kv_gain, page_owner, page_request, queries, cache, lengths):
    cosine, sine = tables()
    anywhere = pl.BlockSpec(memory_space=pl.ANY)
    vmem = pl.BlockSpec(memory_space=pltpu.VMEM)
    smem = pl.BlockSpec(memory_space=pltpu.SMEM)
    sums = pl.pallas_call(
        kernel,
        out_shape=jax.ShapeDtypeStruct((4, 2 * NR, 32, 64), F32),
        in_specs=[anywhere, anywhere, vmem, smem, smem, anywhere, anywhere, smem, vmem, vmem],
        out_specs=vmem,
        scratch_shapes=[
            pltpu.VMEM((TOK, HALF_D), BF16),
            pltpu.VMEM((4, BLK, HALF_D), BF16),
            pltpu.VMEM((4, BLK, TOK), F32),
            pltpu.VMEM((4, BLK, TOK), I16),
            pltpu.VMEM((4, BLK, TOK), I16),
            pltpu.VMEM((4, 1, TOK), F32),
            pltpu.VMEM((4, 1, TOK), F32),
            pltpu.VMEM((KVX, TOK), BF16),
            pltpu.VMEM((3, CAPTOK, KVX), BF16),
            pltpu.VMEM((2, CAPTOK // 2, KVX), BF16),
            pltpu.VMEM((4, 2, CAPTOK, KVX), BF16),
            pltpu.VMEM((1, TOK), I32),
            pltpu.VMEM((NR, 4, 64, KVW), BF16),
            pltpu.VMEM((NR, QROWS, KVX), BF16),
            pltpu.VMEM((2, NR, KVW, CTXD), BF16),
            pltpu.VMEM((NR, QROWS, LATW), F32),
            pltpu.VMEM((NR, QROWS, 128), F32),
            pltpu.VMEM((NR, QROWS, 128), F32),
            pltpu.VMEM((NR, 4, 2, 64, QROWS), I16),
            pltpu.VMEM((NR, 3, 1, QROWS), F32),
            pltpu.VMEM((NR, 6, 64, QROWS), I16),
            pltpu.VMEM((NR, 6, 3, 1, QROWS), F32),
            pltpu.VMEM((NR, 2, 64, QROWS), I16),
            pltpu.VMEM((NR, 2, 3, 1, QROWS), F32),
            pltpu.VMEM((NR, 2, 64, QROWS), I16),
            pltpu.VMEM((NR, 2, 3, 1, QROWS), F32),
            pltpu.VMEM((NR, 64, QROWS), I16),
            pltpu.VMEM((NR, 3, 1, QROWS), F32),
            pltpu.VMEM((NR, 2, 4, 32, 64), F32),
            pltpu.SemaphoreType.DMA((7,)),
            pltpu.SemaphoreType.DMA((LINKS,)),
            pltpu.SemaphoreType.DMA((LINKS,)),
        ],
        compiler_params=pltpu.CompilerParams(
            collective_id=0, has_side_effects=True, vmem_limit_bytes=56 * 1024 * 1024
        ),
        cost_estimate=pl.CostEstimate(flops=7_500_000_000, bytes_accessed=12_000_000, transcendentals=3_000_000),
    )(
        hidden, kv_down.T, kv_gain.reshape(1, LATW), page_owner.T, page_request, queries, cache.transpose(0, 2, 1), lengths,
        jnp.asarray(cosine), jnp.asarray(sine),
    )
    return sums.transpose(0, 1, 3, 2)


def solution(mesh):
    return jax.shard_map(
        on_device,
        mesh=mesh,
        in_specs=(
            P(("seq", "batch"), "mp"),
            P("mp", "batch"),
            P(),
            P(("seq", "batch"), None),
            P(("seq", "batch")),
            P(None, "batch", "mp", None),
            P("batch", "seq", None),
            P("batch"),
        ),
        out_specs=P(None, "batch", "mp", "seq"),
        check_vma=False,
    )
```

time: 401 us -> 76.3 us (0.19)
  waiting for transfers between devices: 185 us -> 0 us
  blocking collectives: 129 us -> 0 us
  Pallas kernels: 0 us -> 74.2 us
  matrix products: 25.5 us -> 0 us
  other arithmetic: 19.5 us -> 0 us
  local copies, waits for them, and re-layouts: 16.6 us -> 1.87 us
  between operations: 13.2 us -> 0.01 us
  starting transfers between devices: 10.2 us -> 0 us
    psum x2 -> x0, waiting for transfers between devices: 126 us -> none  [the longest x1 89.7 us: on_device(): whole_total, whole_numer = lax.psum((totals, numerator), 'seq')]
    pallas_call x0 -> x1, Pallas kernels: none -> 74.2 us  [on_device(): pl.pallas_call(kernel, out_shape=jax.ShapeDtypeStruct((4, 2 * NR, 32, 64)...]
    psum x1 -> x0, blocking collectives: 65 us -> none  [on_device(): whole_total, whole_numer = lax.psum((totals, numerator), 'seq')]
    pmax x1 -> x0, blocking collectives: 63.9 us -> none  [on_device(): highest = lax.pmax(local_peak, 'seq')]
    all_gather x1 -> x0, waiting for transfers between devices: 42.5 us -> none  [on_device(): lax.all_gather(kv_down, 'batch', axis=1, tiled=True)]
    dot_general x7 -> x0, matrix products: 25.5 us -> none  [the longest x1 7 us: on_device(): jnp.einsum('srhk,rtk->srht', queries, cache, preferred_element_type=jnp.f...]
    all_to_all x2 -> x0, waiting for transfers between devices: 15.3 us -> none  [the longest x1 15.3 us: on_device(): lax.all_to_all(packed, 'batch', split_axis=0, concat_axis=0, tiled=True)]
    all_to_all x2 -> x0, starting transfers between devices: 10.1 us -> none  [the longest x1 5.86 us: on_device(): lax.all_to_all(labels, 'batch', split_axis=0, concat_axis=0, tiled=True)]
  transfers between devices with their start and end apart: 5 -> 0, of which waited for: 4 -> 0; matrix products, arithmetic and copies ran while one was open for 8% -> 0% of each run, Pallas kernels for 0% -> 0%
where the time goes in v1:
time: 76.3 us; the launch traced here: 76.1 us
  Pallas kernels  74.2 us (97%)
  local copies, waits for them, and re-layouts  1.87 us (2%)
    pallas_call x1, Pallas kernels, on_device(): pl.pallas_call(kernel, out_shape=jax.ShapeDtypeStruct((4, 2 * NR, 32, 64)...  74.2 us
    unnamed x1, local copies, waits for them, and re-layouts  1.87 us

profile of v1, /device:TPU:1, one launch (start us, length us, event | category | flops | bytes accessed | tf_op | source)
XLA Modules:
  0.0 76.1 jit_solution(13382821476867715006)
XLA Ops:
  0.0 74.2 %shard_map.100 = f32[4,8,32,64]{3,2,1,0:T(8,128)} custom-call(bf16[384,3584]{1,0:T(8,128)(2,1)} %hidden.1, bf16[144,3584]{1,0:T(8,128)(2,1)} %bitcast.7, f32[1,512]{1,0:T(1,128)} %bitcast.8, s32[1,24]{1,0:T(1,128)} %bitcast.9, s32[24]{0:T(128)} %request.1, bf16[4,8,64,576]{3,2,1,0:T(8,128)(2,1)} %queries.1, bf16[8,576,512]{2,1,0:T(8,128)(2,1)} %bitcast.6, ...), custom_call_target="tpu_custom_call" | custom-call | flops 7500000256 | bytes 12000000 | tf_op jit(solution)/shard_map/pallas_call | solution.py:471
  74.2 1.9 %copy.12 = f32[4,8,64,32]{2,3,1,0:T(8,128)} copy(f32[4,8,64,32]{2,3,1,0:T(8,128)} %bitcast.5) | data formatting | bytes 524288

commit v2 on v1

--- a/solution.py
+++ b/solution.py
@@ -11,7 +11,8 @@
 
 eps_norm = 1e-06
 score_scale = 192.0 ** (-0.5)
-log2_scale = score_scale * 1.4426950408889634
+log2_e = 1.4426950408889634
+log2_scale = score_scale * log2_e
 rope_base = 10000.0
 masked_value = -1e30
 floor_value = -1e29
@@ -27,6 +28,7 @@
 QROWS = 256
 CTXD = 512
 NR = 4
+PAIRS = ((0, 1), (2, 3))
 
 
 def nt(a, b):
@@ -41,7 +43,7 @@
     hidden, kv_down, gain, owner, request, queries, cache, lengths, cosine, sine,
     out,
     hid, kvt, lat, mps, mpr, mss, msr, rows, packed, relay, arr, tok,
-    qraw, qbuf, kbuf, acc, ms, ls, osend, ostat, ybuf, ystat, rsend, rstat, mbuf, mstat, xbuf, xstat, fin,
+    qraw, qbuf, kbuf, esend, estat, ebuf, efrom, acc, ms, ls, osend, ostat, ybuf, ystat, rsend, rstat, mbuf, mstat, fbuf, fstat,
     loc, send, recv,
 ):
     s, b, p = lax.axis_index("seq"), lax.axis_index("batch"), lax.axis_index("mp")
@@ -58,13 +60,16 @@
     dev_yp = (lax.rem(y + 1, 4) * 4 + in_y, b, p)
     dev_ym = (lax.rem(y + 3, 4) * 4 + in_y, b, p)
     dev_x = (s + 2 - 4 * xh, b, p)
+    dev_x_sib = (sib + 2 - 4 * xh, b, p)
 
     used = [0]
     started = []
 
     def link(src, dst, dev):
-        i = used[0]
         used[0] += 1
+        return link_at(used[0] - 1, src, dst, dev)
+
+    def link_at(i, src, dst, dev):
         return pltpu.make_async_remote_copy(
             src_ref=src, dst_ref=dst, send_sem=send.at[i], recv_sem=recv.at[i],
             device_id=dev, device_id_type=MESH,
@@ -76,7 +81,8 @@
 
     def code(value, axis):
         most = jnp.max(jnp.abs(value), axis=axis, keepdims=True)
-        return jnp.round(value * (code_top / jnp.maximum(most, 1e-30))), most * (1.0 / code_top)
+        most = jnp.maximum(most, 1e-25)
+        return jnp.round(value * (code_top / most)), most * (1.0 / code_top)
 
     def to_code(value):
         return value.astype(I32).astype(I16)
@@ -98,17 +104,16 @@
     load_hid.start()
     load_q = []
     for step in range(4):
-        load_q.append(pltpu.make_async_copy(queries.at[step, pl.ds(c * NR, NR)], qraw.at[:, step], loc.at[2 + step]))
+        load_q.append(pltpu.make_async_copy(queries.at[step], qraw.at[:, step], loc.at[2 + step]))
         load_q[-1].start()
-    load_cache = pltpu.make_async_copy(cache.at[pl.ds(c * NR, NR)], kbuf.at[0], loc.at[6])
+    load_cache = pltpu.make_async_copy(cache, kbuf, loc.at[6])
     load_cache.start()
 
     barrier = pltpu.get_barrier_semaphore()
-    for dev in (dev_zp, dev_zm, dev_zz, dev_mp, dev_sib, dev_yp, dev_ym, dev_x):
+    for dev in (dev_zp, dev_zm, dev_zz, dev_mp, dev_sib, dev_yp, dev_ym, dev_x, dev_x_sib):
         pl.semaphore_signal(barrier, inc=1, device_id=dev, device_id_type=MESH)
 
-    load_kv.wait()
-    pl.semaphore_wait(barrier, 8)
+    pl.semaphore_wait(barrier, 9)
 
     base = c * (HALF_D // 2)
 
@@ -118,18 +123,19 @@
     def kv_link(slot, to_slot, at, dev):
         return link(kvt.at[slot, :, at], kvt.at[to_slot, :, at], dev)
 
+    def first_link(to_slot, at, dev):
+        return link(kv_down.at[:, at], kvt.at[to_slot, :, at], dev)
+
     def part_of(k, first=0, size=SHARE):
         return lanes(lax.rem(y + k, 4) * SHARE + first, size)
 
     low, high = lanes(4 * SHARE, DIRECT), lanes(4 * SHARE + DIRECT, DIRECT)
     mine = part_of(0)
-    s_p, s_m = kv_link(0, 1, mine, dev_zp), kv_link(0, 2, mine, dev_zm)
-    d_p0, d_m1 = kv_link(0, 1, low, dev_zp), kv_link(0, 2, high, dev_zm)
-    d_p1, d_m0 = kv_link(0, 1, high, dev_zp), kv_link(0, 2, low, dev_zm)
-    for copy in (s_p, s_m, d_p0, d_m1, d_p1, d_m0):
+    s_p, s_m = first_link(1, mine, dev_zp), first_link(2, mine, dev_zm)
+    d_p0, d_m1 = first_link(1, low, dev_zp), first_link(2, high, dev_zm)
+    d_p1, d_m0 = first_link(1, high, dev_zp), first_link(2, low, dev_zm)
+    for copy in (s_p, s_m, d_p0, d_m1):
         go(copy)
-    cache_out = link(cache.at[pl.ds((1 - c) * NR, NR)], kbuf.at[1], dev_sib)
-    go(cache_out)
     sf_p, sf_m = (
         kv_link(1, 3, part_of(0, 0, SHARE // 2), dev_zp),
         kv_link(2, 3, part_of(0, SHARE // 2, SHARE // 2), dev_zm),
@@ -137,14 +143,12 @@
     df_p, df_m = kv_link(1, 3, low, dev_zp), kv_link(2, 3, high, dev_zm)
     near_p = [None] + [kv_link(slot, slot, mine, dev_yp) for slot in (1, 2, 3)]
     near_m = [None] + [kv_link(slot, slot, mine, dev_ym) for slot in (1, 2, 3)]
-    far = [
-        None,
-        [kv_link(1, 1, part_of(3), dev_yp)],
-        [kv_link(2, 2, part_of(1), dev_ym)],
-        [
-            kv_link(3, 3, part_of(3, 0, SHARE // 2), dev_yp),
-            kv_link(3, 3, part_of(1, SHARE // 2, SHARE // 2), dev_ym),
-        ],
+    far = [None] + [
+        (
+            kv_link(slot, slot, part_of(3, 0, SHARE // 2), dev_yp),
+            kv_link(slot, slot, part_of(1, SHARE // 2, SHARE // 2), dev_ym),
+        )
+        for slot in (1, 2, 3)
     ]
     share_s = [None] + [kv_link(slot, slot, lanes(0, 4 * SHARE), dev_sib) for slot in (1, 2, 3)]
     share_d = [None] + [kv_link(slot, slot, lanes(4 * SHARE, 2 * DIRECT), dev_sib) for slot in (1, 2, 3)]
@@ -199,22 +203,49 @@
             most = jnp.maximum(most, score[:, j * 128:j * 128 + 128])
         return most
 
-    def resident(r, carry):
-        q = qbuf[r, :, :KVW]
-        length = lengths[c * NR + r]
-        at = lax.broadcasted_iota(I32, (1, CTXD), 1)
-        score0 = jnp.where(at + s * CTXD < length, nn(q, kbuf[0, r]), masked_value)
-        score1 = jnp.where(at + sib * CTXD < length, nn(q, kbuf[1, r]), masked_value)
-        top = jnp.max(jnp.maximum(peak(score0), peak(score1)), axis=1, keepdims=True)
-        top = jnp.maximum(top, floor_value)
-        w0 = weigh(score0, top)
-        w1 = weigh(score1, top)
-        acc[r] = nt(w0.astype(BF16), kbuf[0, r, :LATW, :]) + nt(w1.astype(BF16), kbuf[1, r, :LATW, :])
+    lane = lax.broadcasted_iota(I32, (QROWS, 128), 1)
+
+    def put_columns(stat_ref, top, total, scale):
+        stat = jnp.transpose(jnp.where(lane == 0, top * log2_scale, scale))
+        stat_ref[0] = stat[0:1]
+        stat_ref[1] = jnp.sum(jnp.transpose(total), axis=0, keepdims=True)
+        stat_ref[2] = stat[1:2]
+
+    def resident(pair, half):
+        at = lax.broadcasted_iota(I32, (1, CTXD), 1) + s * CTXD
+        scores = [
+            jnp.where(at < lengths[half * NR + r], nn(qbuf[half * NR + r, :, :KVW], kbuf[half * NR + r]), masked_value)
+            for r in pair
+        ]
+        weights = []
+        for score in scores:
+            top = jnp.maximum(jnp.max(peak(score), axis=1, keepdims=True), floor_value)
+            w = weigh(score, top)
+            weights.append((w.astype(BF16), jnp.broadcast_to(top, (QROWS, 128)), fold(w)))
+        return [
+            (nt(w, kbuf[half * NR + r, :LATW, :]), top, total) for r, (w, top, total) in zip(pair, weights)
+        ]
+
+    def resident_own(i, carry):
+        for r, state in zip((2 * i, 2 * i + 1), resident((2 * i, 2 * i + 1), c)):
+            acc[r], ms[r], ls[r] = state
+        return carry
+
+    def add_other(r, carry):
+        row = lax.broadcasted_iota(I32, (128, QROWS), 0)
+        stat = jnp.where(row == 0, efrom[r, 0], jnp.where(row == 1, efrom[r, 1], efrom[r, 2]))
+        stat = jnp.transpose(stat)
+        top2, total2, scale2 = stat[:, 0:1] * (1.0 / log2_scale), stat[:, 1:2], stat[:, 2:3]
+        old = ms[r][:, :1]
+        top = jnp.maximum(old, top2)
+        keep, gain2 = jnp.exp2((old - top) * log2_scale), jnp.exp2((top2 - top) * log2_scale)
+        acc[r] = acc[r] * keep + from_code(ebuf[r]) * (gain2 * scale2)
         ms[r] = jnp.broadcast_to(top, (QROWS, 128))
-        ls[r] = fold(w0) + fold(w1)
+        ls[r] = ls[r] * keep + jnp.where(lane == 0, gain2 * total2, 0.0)
         return carry
 
     load_hid.wait()
+    load_kv.wait()
     s_p.wait_recv()
     go(sf_p)
     go(near_p[1])
@@ -223,16 +254,27 @@
     go(sf_m)
     go(near_p[2])
     go(near_m[2])
+    go(d_p1)
+    go(d_m0)
     send_part(0, nt(kvt[0], hid[...]), m_copies[0])
 
-    near_p[1].wait_recv()
-    go(far[1][0])
-    near_m[2].wait_recv()
-    go(far[2][0])
     d_p0.wait_recv()
     go(df_p)
     d_m1.wait_recv()
     go(df_m)
+
+    def pass_on(slot):
+        near_p[slot].wait_recv()
+        go(far[slot][0])
+        near_m[slot].wait_recv()
+        go(far[slot][1])
+
+    def swap_shared(slot):
+        far[slot][0].wait_recv()
+        far[slot][1].wait_recv()
+        go(share_s[slot])
+
+    pass_on(1)
     sf_p.wait_recv()
     sf_m.wait_recv()
     go(near_p[3])
@@ -241,46 +283,70 @@
     for copy in load_q:
         copy.wait()
     load_cache.wait()
-    cache_out.wait_recv()
     label_at = lax.broadcasted_iota(I32, (QROWS, LABELS), 1)
-    for r in range(NR):
+
+    def fill(r, carry):
         qbuf[r, :, :KVW] = qraw[r].reshape(QROWS, KVW)
-        qbuf[r, :, KVW:] = jnp.where(label_at == c * NR + r + 1, 0.0, masked_value).astype(BF16)
-    lax.fori_loop(0, 1, resident, 0)
-
+        qbuf[r, :, KVW:] = jnp.where(label_at == r + 1, 0.0, masked_value).astype(BF16)
+        return carry
+
+    def resident_other(i, carry):
+        for r, (value, top, total) in zip((2 * i, 2 * i + 1), resident((2 * i, 2 * i + 1), 1 - c)):
+            coded, scale = code(value, 1)
+            esend[r] = to_code(coded)
+            put_columns(estat.at[r], top, total, scale)
+        return carry
+
+    lax.fori_loop(0, 2 * NR, fill, 0)
+    lax.fori_loop(0, 1, resident_other, 0)
+
+    pass_on(2)
     d_p1.wait_recv()
     go(share_d[1])
     d_m0.wait_recv()
     go(share_d[2])
-    near_m[1].wait_recv()
-    far[1][0].wait_recv()
-    go(share_s[1])
-    near_p[2].wait_recv()
-    far[2][0].wait_recv()
-    go(share_s[2])
-    near_p[3].wait_recv()
-    go(far[3][0])
-    near_m[3].wait_recv()
-    go(far[3][1])
-    lax.fori_loop(1, 2, resident, 0)
-
+    swap_shared(1)
+    swap_shared(2)
+
+    def over_lanes(slots, starts, size, at):
+        keys = slice(slots[0], slots[-1] + 1)
+        rows_at = len(slots) * BLK
+        return sum(
+            nt(kvt[keys, :, start:start + size].reshape(rows_at, size), hid[at, start:start + size]) for start in starts
+        )
+
+    direct_at = ((4 * SHARE, HALF_D // 2 + 4 * SHARE), 2 * DIRECT)
+    shared_at = ((0, HALF_D // 2), 4 * SHARE)
+    whole_at = slice(None)
+    share_d[1].wait_recv()
+    share_d[2].wait_recv()
+    both = over_lanes((1, 2), *direct_at, whole_at)
+    lat[origin[1]] = both[:BLK]
+    lat[origin[2]] = both[BLK:]
+    pass_on(3)
+    for slot in (1, 2):
+        share_s[slot].wait_recv()
+        send_part(slot, lat[origin[slot]] + over_lanes((slot,), *shared_at, whole_at), m_copies[slot])
     df_p.wait_recv()
     df_m.wait_recv()
     go(share_d[3])
-    for slot in (1, 2):
-        share_d[slot].wait_recv()
-        share_s[slot].wait_recv()
-    both = nt(kvt[1:3].reshape(2 * BLK, HALF_D), hid[...])
-    for slot in (1, 2):
-        send_part(slot, both[(slot - 1) * BLK:slot * BLK], m_copies[slot])
-
-    far[3][0].wait_recv()
-    far[3][1].wait_recv()
-    go(share_s[3])
+    swap_shared(3)
     share_d[3].wait_recv()
+    lat[origin[3]] = over_lanes((3,), *direct_at, whole_at)
     share_s[3].wait_recv()
     for i, at in enumerate(tails):
-        send_part(3, nt(kvt[3], hid[at, :]), m_copies[3 + i], at)
+        send_part(3, lat[origin[3], :, at] + over_lanes((3,), *shared_at, at), m_copies[3 + i], at)
+
+    lax.fori_loop(1, 2, resident_other, 0)
+    e_copies = [
+        (link(esend.at[r], ebuf.at[r], dev_sib), link(estat.at[r], efrom.at[r], dev_sib)) for r in range(NR)
+    ]
+    for pair in e_copies:
+        go_pair(pair)
+    lax.fori_loop(0, 2, resident_own, 0)
+    for pair in e_copies:
+        wait_pair(pair)
+    lax.fori_loop(0, NR, add_other, 0)
 
     for slot in range(4):
         for pair in m_copies[slot:] if slot == 3 else m_copies[slot:slot + 1]:
@@ -328,44 +394,43 @@
     arr[0, c] = pack_for(b)
     go(a_share[0])
 
-    def pages_step(r, slots):
-        q = qbuf[r]
-        old = ms[r][:, :1]
-        scores = [nt(q, arr[slot].reshape(2 * CAPTOK, KVX)) for slot in slots]
-        most = peak(scores[0])
-        for score in scores[1:]:
-            most = jnp.maximum(most, peak(score))
-        top = jnp.maximum(old, jnp.max(most, axis=1, keepdims=True))
-        shrink = jnp.exp2((old - top) * log2_scale)
-        total = ls[r] * shrink
-        value = acc[r] * shrink
-        for slot, score in zip(slots, scores):
+    def pages_step(pair, first, last):
+        keys = arr[first:last + 1].reshape((last + 1 - first) * 2 * CAPTOK, KVX)
+        scores = [nt(qbuf[c * NR + r], keys) for r in pair]
+        weights = []
+        for r, score in zip(pair, scores):
+            old = ms[r][:, :1]
+            top = jnp.maximum(old, jnp.max(peak(score), axis=1, keepdims=True))
+            shrink = jnp.exp2((old - top) * log2_scale)
             w = weigh(score, top)
-            total = total + fold(w)
-            value = value + nn(w.astype(BF16), arr[slot].reshape(2 * CAPTOK, KVX)[:, :LATW])
-        return value, jnp.broadcast_to(top, (QROWS, 128)), total
-
-    def pages_of(slots):
-        def body(r, carry):
-            acc[r], ms[r], ls[r] = pages_step(r, slots)
+            weights.append((w.astype(BF16), shrink, top, ls[r] * shrink + fold(w)))
+        return [
+            (acc[r] * shrink + nn(w, keys[:, :LATW]), jnp.broadcast_to(top, (QROWS, 128)), total)
+            for r, (w, shrink, top, total) in zip(pair, weights)
+        ]
+
+    def pages_of(first, last):
+        def body(i, carry):
+            pair = (2 * i, 2 * i + 1)
+            for r, state in zip(pair, pages_step(pair, first, last)):
+                acc[r], ms[r], ls[r] = state
             return carry
 
-        return body
+        lax.fori_loop(0, 2, body, 0)
 
     a_r0.wait_recv()
     go(a_f0)
     a_r1.wait_recv()
     go(a_f1)
-    lax.fori_loop(2, NR, resident, 0)
     a_share[0].wait_recv()
-    lax.fori_loop(0, NR, pages_of((0,)), 0)
+    pages_of(0, 0)
     a_p.wait_recv()
     go(a_share[1])
     a_m.wait_recv()
     go(a_share[2])
     a_share[1].wait_recv()
     a_share[2].wait_recv()
-    lax.fori_loop(0, NR, pages_of((1, 2)), 0)
+    pages_of(1, 2)
     a_f0.wait_recv()
     go(a_share3[0])
     a_f1.wait_recv()
@@ -380,20 +445,20 @@
         value, total = 0.0, 0.0
         for coded, stat in parts:
             factor = jnp.exp2(stat[0] - top)
-            value = value + from_code(coded) * (factor * stat[2])
+            value = value + from_code(coded) * factor
             total = total + factor * stat[1]
         return value, top, total
 
     def put(coded_ref, stat_ref, value, top, total):
         coded, scale = code(value, 0)
-        coded_ref[...] = to_code(coded)
-        stat_ref[0] = top
-        stat_ref[1] = total
-        stat_ref[2] = scale
+        coded_ref[...] = to_code(coded).reshape(coded_ref.shape)
+        stat_ref[0] = top + jnp.log(scale) * log2_e
+        stat_ref[1] = total / scale
 
     yp, ym, yy = lax.rem(y + 1, 4), lax.rem(y + 3, 4), lax.rem(y + 2, 4)
-    y_copies = []
-    for r in range(NR):
+    first_y = used[0]
+
+    def y_pair(r, k):
         pairs = (
             (osend.at[r, yy, 0], ostat.at[r], 0, dev_yp),
             (osend.at[r, yy, 1], ostat.at[r], 1, dev_ym),
@@ -402,58 +467,80 @@
             (rsend.at[r, 0], rstat.at[r, 0], 4, dev_yp),
             (rsend.at[r, 1], rstat.at[r, 1], 5, dev_ym),
         )
-        y_copies.append([
-            (link(data, ybuf.at[r, k], dev), link(stat, ystat.at[r, k], dev)) for data, stat, k, dev in pairs
-        ])
-
-    lane = lax.broadcasted_iota(I32, (QROWS, 128), 1)
+        data, stat, _, dev = pairs[k]
+        return (
+            link_at(first_y + 18 * r + 2 * k, data, ybuf.at[r, k], dev),
+            link_at(first_y + 18 * r + 2 * k + 1, stat, ystat.at[r, k], dev),
+        )
+
+    def last_pair(r, k):
+        half, core, dev = ((1 - xh, c, dev_x), (1 - xh, 1 - c, dev_x_sib), (xh, 1 - c, dev_sib))[k]
+        return (
+            link_at(first_y + 18 * r + 12 + 2 * k, mbuf.at[r, half, core], fbuf.at[r, k], dev),
+            link_at(first_y + 18 * r + 13 + 2 * k, mstat.at[r, half], fstat.at[r, k], dev),
+        )
+
+    def start_pair(pair):
+        pair[0].start()
+        pair[1].start()
+
     for r in range(NR):
-        value, top, total = pages_step(r, (3,))
+        value, top, total = pages_step((r,), 3, 3)[0]
         coded, scale = code(value, 1)
         osend[r] = to_code(jnp.transpose(coded)).reshape(4, 2, 64, QROWS)
-        stat = jnp.transpose(jnp.where(lane == 0, top * log2_scale, scale))
+        stat = jnp.transpose(jnp.where(lane == 0, top * log2_scale + jnp.log(scale) * log2_e, 1.0 / scale))
         ostat[r, 0] = stat[0:1]
-        ostat[r, 1] = jnp.sum(jnp.transpose(total), axis=0, keepdims=True)
-        ostat[r, 2] = stat[1:2]
+        ostat[r, 1] = jnp.sum(jnp.transpose(total), axis=0, keepdims=True) * stat[1:2]
         for k in range(4):
-            go_pair(y_copies[r][k])
-    for r in range(NR):
+            start_pair(y_pair(r, k))
+
+    def relay_sums(r, carry):
         for k, to in ((0, yp), (1, ym)):
-            wait_pair(y_copies[r][k])
+            wait_pair(y_pair(r, k))
             put(rsend.at[r, k], rstat.at[r, k], *merge([
                 (osend[r, to, k], ostat[r]), (ybuf[r, k], ystat[r, k]),
             ]))
-            go_pair(y_copies[r][4 + k])
-    x_copies = []
-    for r in range(NR):
+            start_pair(y_pair(r, 4 + k))
+        return carry
+
+    def sums_over_y(r, carry):
         for k in range(2, 6):
-            wait_pair(y_copies[r][k])
+            wait_pair(y_pair(r, k))
         for h, (one, two) in enumerate(((3, 4), (2, 5))):
             put(mbuf.at[r, h], mstat.at[r, h], *merge([
                 (osend[r, y, h], ostat[r]), (ybuf[r, one], ystat[r, one]), (ybuf[r, two], ystat[r, two]),
             ]))
-        x_copies.append((
-            link(mbuf.at[r, 1 - xh], xbuf.at[r], dev_x), link(mstat.at[r, 1 - xh], xstat.at[r], dev_x),
-        ))
-        go_pair(x_copies[r])
-    c_copies = []
-    for r in range(NR):
-        wait_pair(x_copies[r])
-        value, _, total = merge([(mbuf[r, xh], mstat[r, xh]), (xbuf[r], xstat[r])])
-        value = value / total
-        for core in range(2):
+        for k in (1, 0, 2):
+            start_pair(last_pair(r, k))
+        return carry
+
+    def last_sums(r, carry):
+        for k in range(3):
+            wait_pair(last_pair(r, k))
+        own, other = c * NR + r, (1 - c) * NR + r
+        for request, parts in (
+            (own, [(mbuf[r, xh, c], mstat[r, xh]), (fbuf[r, 0], fstat[r, 0])]),
+            (other, [(fbuf[r, 2], fstat[r, 2]), (fbuf[r, 1], fstat[r, 1])]),
+        ):
+            value, _, total = merge(parts)
+            value = value / total
             for step in range(4):
-                fin[r, core, step] = value[32 * core:32 * core + 32, 64 * step:64 * step + 64]
-        c_copies.append(link(fin.at[r, 1 - c], out.at[:, c * NR + r], dev_sib))
-        go(c_copies[r])
-        out[:, c * NR + r] = fin[r, c]
-    for copy in c_copies:
-        copy.wait_recv()
+                out[step, request] = value[:, 64 * step:64 * step + 64]
+        return carry
+
+    def finish(r, carry):
+        for pair in [y_pair(r, k) for k in range(6)] + [last_pair(r, k) for k in range(3)]:
+            pair[0].wait_send()
+            pair[1].wait_send()
+        return carry
+
+    for stage in (relay_sums, sums_over_y, last_sums, finish):
+        lax.fori_loop(0, NR, stage, 0)
     for copy in started:
         copy.wait_send()
 
 
-LINKS = 136
+LINKS = 144
 
 
 def tables():
@@ -486,23 +573,26 @@
             pltpu.VMEM((2, CAPTOK // 2, KVX), BF16),
             pltpu.VMEM((4, 2, CAPTOK, KVX), BF16),
             pltpu.VMEM((1, TOK), I32),
-            pltpu.VMEM((NR, 4, 64, KVW), BF16),
-            pltpu.VMEM((NR, QROWS, KVX), BF16),
-            pltpu.VMEM((2, NR, KVW, CTXD), BF16),
+            pltpu.VMEM((2 * NR, 4, 64, KVW), BF16),
+            pltpu.VMEM((2 * NR, QROWS, KVX), BF16),
+            pltpu.VMEM((2 * NR, KVW, CTXD), BF16),
+            pltpu.VMEM((NR, QROWS, LATW), I16),
+            pltpu.VMEM((NR, 3, 1, QROWS), F32),
+            pltpu.VMEM((NR, QROWS, LATW), I16),
+            pltpu.VMEM((NR, 3, 1, QROWS), F32),
             pltpu.VMEM((NR, QROWS, LATW), F32),
             pltpu.VMEM((NR, QROWS, 128), F32),
             pltpu.VMEM((NR, QROWS, 128), F32),
             pltpu.VMEM((NR, 4, 2, 64, QROWS), I16),
-            pltpu.VMEM((NR, 3, 1, QROWS), F32),
+            pltpu.VMEM((NR, 2, 1, QROWS), F32),
             pltpu.VMEM((NR, 6, 64, QROWS), I16),
-            pltpu.VMEM((NR, 6, 3, 1, QROWS), F32),
+            pltpu.VMEM((NR, 6, 2, 1, QROWS), F32),
             pltpu.VMEM((NR, 2, 64, QROWS), I16),
-            pltpu.VMEM((NR, 2, 3, 1, QROWS), F32),
-            pltpu.VMEM((NR, 2, 64, QROWS), I16),
-            pltpu.VMEM((NR, 2, 3, 1, QROWS), F32),
-            pltpu.VMEM((NR, 64, QROWS), I16),
-            pltpu.VMEM((NR, 3, 1, QROWS), F32),
-            pltpu.VMEM((NR, 2, 4, 32, 64), F32),
+            pltpu.VMEM((NR, 2, 2, 1, QROWS), F32),
+            pltpu.VMEM((NR, 2, 2, 32, QROWS), I16),
+            pltpu.VMEM((NR, 2, 2, 1, QROWS), F32),
+            pltpu.VMEM((NR, 3, 32, QROWS), I16),
+            pltpu.VMEM((NR, 3, 2, 1, QROWS), F32),
             pltpu.SemaphoreType.DMA((7,)),
             pltpu.SemaphoreType.DMA((LINKS,)),
             pltpu.SemaphoreType.DMA((LINKS,)),

time: 76.3 us -> 73.6 us (0.965)
  Pallas kernels: 74.2 us -> 71.5 us
    pallas_call x1, Pallas kernels: 74.2 us -> 71.5 us  [on_device(): pl.pallas_call(kernel, out_shape=jax.ShapeDtypeStruct((4, 2 * NR, 32, 64)...]
where the time goes in v2:
time: 73.6 us; the launch traced here: 73.4 us
  Pallas kernels  71.5 us (97%)
  local copies, waits for them, and re-layouts  1.87 us (3%)
    pallas_call x1, Pallas kernels, on_device(): pl.pallas_call(kernel, out_shape=jax.ShapeDtypeStruct((4, 2 * NR, 32, 64)...  71.5 us
    unnamed x1, local copies, waits for them, and re-layouts  1.87 us

profile of v2, /device:TPU:1, one launch (start us, length us, event | category | flops | bytes accessed | tf_op | source)
XLA Modules:
  0.0 73.4 jit_solution(3232559528032251762)
XLA Ops:
  0.0 71.5 %shard_map.100 = f32[4,8,32,64]{3,2,1,0:T(8,128)} custom-call(bf16[384,3584]{1,0:T(8,128)(2,1)} %hidden.1, bf16[144,3584]{1,0:T(8,128)(2,1)} %bitcast.7, f32[1,512]{1,0:T(1,128)} %bitcast.8, s32[1,24]{1,0:T(1,128)} %bitcast.9, s32[24]{0:T(128)} %request.1, bf16[4,8,64,576]{3,2,1,0:T(8,128)(2,1)} %queries.1, bf16[8,576,512]{2,1,0:T(8,128)(2,1)} %bitcast.6, ...), custom_call_target="tpu_custom_call" | custom-call | flops 7500000256 | bytes 12000000 | tf_op jit(solution)/shard_map/pallas_call | solution.py:558
  71.5 1.9 %copy.12 = f32[4,8,64,32]{2,3,1,0:T(8,128)} copy(f32[4,8,64,32]{2,3,1,0:T(8,128)} %bitcast.5) | data formatting | bytes 524288

commit v3 on v2

--- a/solution.py
+++ b/solution.py
@@ -256,7 +256,7 @@
     go(near_m[2])
     go(d_p1)
     go(d_m0)
-    send_part(0, nt(kvt[0], hid[...]), m_copies[0])
+    send_part(0, jnp.transpose(nt(hid[...], kvt[0])), m_copies[0])
 
     d_p0.wait_recv()
     go(df_p)
@@ -308,34 +308,28 @@
     swap_shared(1)
     swap_shared(2)
 
-    def over_lanes(slots, starts, size, at):
-        keys = slice(slots[0], slots[-1] + 1)
-        rows_at = len(slots) * BLK
-        return sum(
-            nt(kvt[keys, :, start:start + size].reshape(rows_at, size), hid[at, start:start + size]) for start in starts
-        )
+    for slot in (1, 2):
+        share_d[slot].wait_recv()
+        share_s[slot].wait_recv()
+        send_part(slot, jnp.transpose(nt(hid[...], kvt[slot])), m_copies[slot])
+        if slot == 1:
+            pass_on(3)
+
+    def over_lanes(starts, size, at):
+        part = sum(nt(hid[at, start:start + size], kvt[3, :, start:start + size]) for start in starts)
+        return jnp.transpose(part)
 
     direct_at = ((4 * SHARE, HALF_D // 2 + 4 * SHARE), 2 * DIRECT)
     shared_at = ((0, HALF_D // 2), 4 * SHARE)
-    whole_at = slice(None)
-    share_d[1].wait_recv()
-    share_d[2].wait_recv()
-    both = over_lanes((1, 2), *direct_at, whole_at)
-    lat[origin[1]] = both[:BLK]
-    lat[origin[2]] = both[BLK:]
-    pass_on(3)
-    for slot in (1, 2):
-        share_s[slot].wait_recv()
-        send_part(slot, lat[origin[slot]] + over_lanes((slot,), *shared_at, whole_at), m_copies[slot])
     df_p.wait_recv()
     df_m.wait_recv()
     go(share_d[3])
     swap_shared(3)
     share_d[3].wait_recv()
-    lat[origin[3]] = over_lanes((3,), *direct_at, whole_at)
+    lat[origin[3]] = over_lanes(*direct_at, slice(None))
     share_s[3].wait_recv()
     for i, at in enumerate(tails):
-        send_part(3, lat[origin[3], :, at] + over_lanes((3,), *shared_at, at), m_copies[3 + i], at)
+        send_part(3, lat[origin[3], :, at] + over_lanes(*shared_at, at), m_copies[3 + i], at)
 
     lax.fori_loop(1, 2, resident_other, 0)
     e_copies = [

time: 73.6 us -> 75.4 us (1.024)
  Pallas kernels: 71.5 us -> 73.3 us
    pallas_call x1, Pallas kernels: 71.5 us -> 73.3 us  [on_device(): pl.pallas_call(kernel, out_shape=jax.ShapeDtypeStruct((4, 2 * NR, 32, 64)...]
where the time goes in v3:
time: 75.4 us; the launch traced here: 75.2 us
  Pallas kernels  73.3 us (97%)
  local copies, waits for them, and re-layouts  1.87 us (2%)
    pallas_call x1, Pallas kernels, on_device(): pl.pallas_call(kernel, out_shape=jax.ShapeDtypeStruct((4, 2 * NR, 32, 64)...  73.3 us
    unnamed x1, local copies, waits for them, and re-layouts  1.87 us

profile of v3, /device:TPU:1, one launch (start us, length us, event | category | flops | bytes accessed | tf_op | source)
XLA Modules:
  0.0 75.2 jit_solution(8646006138686091195)
XLA Ops:
  0.0 73.3 %shard_map.100 = f32[4,8,32,64]{3,2,1,0:T(8,128)} custom-call(bf16[384,3584]{1,0:T(8,128)(2,1)} %hidden.1, bf16[144,3584]{1,0:T(8,128)(2,1)} %bitcast.7, f32[1,512]{1,0:T(1,128)} %bitcast.8, s32[1,24]{1,0:T(1,128)} %bitcast.9, s32[24]{0:T(128)} %request.1, bf16[4,8,64,576]{3,2,1,0:T(8,128)(2,1)} %queries.1, bf16[8,576,512]{2,1,0:T(8,128)(2,1)} %bitcast.6, ...), custom_call_target="tpu_custom_call" | custom-call | flops 7500000256 | bytes 12000000 | tf_op jit(solution)/shard_map/pallas_call | solution.py:552
  73.3 1.9 %copy.12 = f32[4,8,64,32]{2,3,1,0:T(8,128)} copy(f32[4,8,64,32]{2,3,1,0:T(8,128)} %bitcast.5) | data formatting | bytes 524288

commit v4 on v3

--- a/solution.py
+++ b/solution.py
@@ -42,7 +42,7 @@
 def kernel(
     hidden, kv_down, gain, owner, request, queries, cache, lengths, cosine, sine,
     out,
-    hid, kvt, lat, mps, mpr, mss, msr, rows, packed, relay, arr, tok,
+    hid, hidt, keyst, kvt, lat, mps, mpr, mss, msr, rows, packed, relay, arr, tok,
     qraw, qbuf, kbuf, esend, estat, ebuf, efrom, acc, ms, ls, osend, ostat, ybuf, ystat, rsend, rstat, mbuf, mstat, fbuf, fstat,
     loc, send, recv,
 ):
@@ -143,12 +143,14 @@
     df_p, df_m = kv_link(1, 3, low, dev_zp), kv_link(2, 3, high, dev_zm)
     near_p = [None] + [kv_link(slot, slot, mine, dev_yp) for slot in (1, 2, 3)]
     near_m = [None] + [kv_link(slot, slot, mine, dev_ym) for slot in (1, 2, 3)]
-    far = [None] + [
-        (
-            kv_link(slot, slot, part_of(3, 0, SHARE // 2), dev_yp),
-            kv_link(slot, slot, part_of(1, SHARE // 2, SHARE // 2), dev_ym),
-        )
-        for slot in (1, 2, 3)
+    far = [
+        None,
+        [kv_link(1, 1, part_of(3), dev_yp)],
+        [kv_link(2, 2, part_of(1), dev_ym)],
+        [
+            kv_link(3, 3, part_of(3, 0, SHARE // 2), dev_yp),
+            kv_link(3, 3, part_of(1, SHARE // 2, SHARE // 2), dev_ym),
+        ],
     ]
     share_s = [None] + [kv_link(slot, slot, lanes(0, 4 * SHARE), dev_sib) for slot in (1, 2, 3)]
     share_d = [None] + [kv_link(slot, slot, lanes(4 * SHARE, 2 * DIRECT), dev_sib) for slot in (1, 2, 3)]
@@ -245,6 +247,13 @@
         return carry
 
     load_hid.wait()
+
+    def turn(j, carry):
+        at = pl.ds(pl.multiple_of(j * 512, 512), 512)
+        hidt[at, :] = jnp.transpose(hid[:, at])
+        return carry
+
+    lax.fori_loop(0, HALF_D // 512, turn, 0)
     load_kv.wait()
     s_p.wait_recv()
     go(sf_p)
@@ -256,25 +265,16 @@
     go(near_m[2])
     go(d_p1)
     go(d_m0)
-    send_part(0, jnp.transpose(nt(hid[...], kvt[0])), m_copies[0])
-
+    send_part(0, nn(kvt[0], hidt[...]), m_copies[0])
+
+    near_p[1].wait_recv()
+    go(far[1][0])
+    near_m[2].wait_recv()
+    go(far[2][0])
     d_p0.wait_recv()
     go(df_p)
     d_m1.wait_recv()
     go(df_m)
-
-    def pass_on(slot):
-        near_p[slot].wait_recv()
-        go(far[slot][0])
-        near_m[slot].wait_recv()
-        go(far[slot][1])
-
-    def swap_shared(slot):
-        far[slot][0].wait_recv()
-        far[slot][1].wait_recv()
-        go(share_s[slot])
-
-    pass_on(1)
     sf_p.wait_recv()
     sf_m.wait_recv()
     go(near_p[3])
@@ -289,6 +289,8 @@
         qbuf[r, :, :KVW] = qraw[r].reshape(QROWS, KVW)
         qbuf[r, :, KVW:] = jnp.where(label_at == r + 1, 0.0, masked_value).astype(BF16)
         return carry
+
+    lax.fori_loop(0, 2 * NR, fill, 0)
 
     def resident_other(i, carry):
         for r, (value, top, total) in zip((2 * i, 2 * i + 1), resident((2 * i, 2 * i + 1), 1 - c)):
@@ -297,46 +299,51 @@
             put_columns(estat.at[r], top, total, scale)
         return carry
 
-    lax.fori_loop(0, 2 * NR, fill, 0)
-    lax.fori_loop(0, 1, resident_other, 0)
-
-    pass_on(2)
-    d_p1.wait_recv()
-    go(share_d[1])
-    d_m0.wait_recv()
-    go(share_d[2])
-    swap_shared(1)
-    swap_shared(2)
-
-    for slot in (1, 2):
-        share_d[slot].wait_recv()
-        share_s[slot].wait_recv()
-        send_part(slot, jnp.transpose(nt(hid[...], kvt[slot])), m_copies[slot])
-        if slot == 1:
-            pass_on(3)
-
-    def over_lanes(starts, size, at):
-        part = sum(nt(hid[at, start:start + size], kvt[3, :, start:start + size]) for start in starts)
-        return jnp.transpose(part)
-
-    direct_at = ((4 * SHARE, HALF_D // 2 + 4 * SHARE), 2 * DIRECT)
-    shared_at = ((0, HALF_D // 2), 4 * SHARE)
-    df_p.wait_recv()
-    df_m.wait_recv()
-    go(share_d[3])
-    swap_shared(3)
-    share_d[3].wait_recv()
-    lat[origin[3]] = over_lanes(*direct_at, slice(None))
-    share_s[3].wait_recv()
-    for i, at in enumerate(tails):
-        send_part(3, lat[origin[3], :, at] + over_lanes(*shared_at, at), m_copies[3 + i], at)
-
-    lax.fori_loop(1, 2, resident_other, 0)
+    lax.fori_loop(0, 2, resident_other, 0)
     e_copies = [
         (link(esend.at[r], ebuf.at[r], dev_sib), link(estat.at[r], efrom.at[r], dev_sib)) for r in range(NR)
     ]
     for pair in e_copies:
         go_pair(pair)
+
+    d_p1.wait_recv()
+    go(share_d[1])
+    d_m0.wait_recv()
+    go(share_d[2])
+    near_m[1].wait_recv()
+    far[1][0].wait_recv()
+    go(share_s[1])
+    near_p[2].wait_recv()
+    far[2][0].wait_recv()
+    go(share_s[2])
+    near_p[3].wait_recv()
+    go(far[3][0])
+    near_m[3].wait_recv()
+    go(far[3][1])
+
+    df_p.wait_recv()
+    df_m.wait_recv()
+    go(share_d[3])
+    share_d[1].wait_recv()
+    share_s[1].wait_recv()
+    send_part(1, nn(kvt[1], hidt[...]), m_copies[1])
+    far[3][0].wait_recv()
+    far[3][1].wait_recv()
+    go(share_s[3])
+    share_d[2].wait_recv()
+    share_s[2].wait_recv()
+    send_part(2, nn(kvt[2], hidt[...]), m_copies[2])
+
+    def over_lanes(starts, size, at):
+        return sum(nn(kvt[3, :, start:start + size], hidt[start:start + size, at]) for start in starts)
+
+    share_d[3].wait_recv()
+    lat[origin[3]] = over_lanes((4 * SHARE, HALF_D // 2 + 4 * SHARE), 2 * DIRECT, slice(None))
+    share_s[3].wait_recv()
+    for i, at in enumerate(tails):
+        send_part(
+            3, lat[origin[3], :, at] + over_lanes((0, HALF_D // 2), 4 * SHARE, at), m_copies[3 + i], at
+        )
     lax.fori_loop(0, 2, resident_own, 0)
     for pair in e_copies:
         wait_pair(pair)
@@ -390,7 +397,7 @@
 
     def pages_step(pair, first, last):
         keys = arr[first:last + 1].reshape((last + 1 - first) * 2 * CAPTOK, KVX)
-        scores = [nt(qbuf[c * NR + r], keys) for r in pair]
+        scores = [nn(qbuf[c * NR + r], keyst[:, :keys.shape[0]]) for r in pair]
         weights = []
         for r, score in zip(pair, scores):
             old = ms[r][:, :1]
@@ -403,7 +410,13 @@
             for r, (w, shrink, top, total) in zip(pair, weights)
         ]
 
+    def turn_keys(first, last):
+        count = (last + 1 - first) * 2 * CAPTOK
+        keyst[:, :count] = jnp.transpose(arr[first:last + 1].reshape(count, KVX))
+
     def pages_of(first, last):
+        turn_keys(first, last)
+
         def body(i, carry):
             pair = (2 * i, 2 * i + 1)
             for r, state in zip(pair, pages_step(pair, first, last)):
@@ -478,6 +491,7 @@
         pair[0].start()
         pair[1].start()
 
+    turn_keys(3, 3)
     for r in range(NR):
         value, top, total = pages_step((r,), 3, 3)[0]
         coded, scale = code(value, 1)
@@ -556,6 +570,8 @@
         out_specs=vmem,
         scratch_shapes=[
             pltpu.VMEM((TOK, HALF_D), BF16),
+            pltpu.VMEM((HALF_D, TOK), BF16),
+            pltpu.VMEM((KVX, 4 * CAPTOK), BF16),
             pltpu.VMEM((4, BLK, HALF_D), BF16),
             pltpu.VMEM((4, BLK, TOK), F32),
             pltpu.VMEM((4, BLK, TOK), I16),

time: 75.4 us -> 72.5 us (0.962)
  Pallas kernels: 73.3 us -> 70.4 us
    pallas_call x1, Pallas kernels: 73.3 us -> 70.4 us  [on_device(): pl.pallas_call(kernel, out_shape=jax.ShapeDtypeStruct((4, 2 * NR, 32, 64)...]
where the time goes in v4:
time: 72.5 us; the launch traced here: 72.3 us
  Pallas kernels  70.4 us (97%)
  local copies, waits for them, and re-layouts  1.87 us (3%)
    pallas_call x1, Pallas kernels, on_device(): pl.pallas_call(kernel, out_shape=jax.ShapeDtypeStruct((4, 2 * NR, 32, 64)...  70.4 us
    unnamed x1, local copies, waits for them, and re-layouts  1.87 us

profile of v4, /device:TPU:1, one launch (start us, length us, event | category | flops | bytes accessed | tf_op | source)
XLA Modules:
  0.0 72.3 jit_solution(6363535497070414866)
XLA Ops:
  0.0 70.4 %shard_map.100 = f32[4,8,32,64]{3,2,1,0:T(8,128)} custom-call(bf16[384,3584]{1,0:T(8,128)(2,1)} %hidden.1, bf16[144,3584]{1,0:T(8,128)(2,1)} %bitcast.7, f32[1,512]{1,0:T(1,128)} %bitcast.8, s32[1,24]{1,0:T(1,128)} %bitcast.9, s32[24]{0:T(128)} %request.1, bf16[4,8,64,576]{3,2,1,0:T(8,128)(2,1)} %queries.1, bf16[8,576,512]{2,1,0:T(8,128)(2,1)} %bitcast.6, ...), custom_call_target="tpu_custom_call" | custom-call | flops 7500000256 | bytes 12000000 | tf_op jit(solution)/shard_map/pallas_call | solution.py:566
  70.4 1.9 %copy.12 = f32[4,8,64,32]{2,3,1,0:T(8,128)} copy(f32[4,8,64,32]{2,3,1,0:T(8,128)} %bitcast.5) | data formatting | bytes 524288

commit v5 on v3

--- a/solution.py
+++ b/solution.py
@@ -24,6 +24,7 @@
 BLK = 144
 SHARE, DIRECT = 256, 384
 CAPTOK = 192
+HALF = CAPTOK // 2
 PAGES, PAGE, CAP = 24, 16, 12
 QROWS = 256
 CTXD = 512
@@ -256,7 +257,7 @@
     go(near_m[2])
     go(d_p1)
     go(d_m0)
-    send_part(0, jnp.transpose(nt(hid[...], kvt[0])), m_copies[0])
+    send_part(0, nt(kvt[0], hid[...]), m_copies[0])
 
     d_p0.wait_recv()
     go(df_p)
@@ -290,15 +291,18 @@
         qbuf[r, :, KVW:] = jnp.where(label_at == r + 1, 0.0, masked_value).astype(BF16)
         return carry
 
-    def resident_other(i, carry):
-        for r, (value, top, total) in zip((2 * i, 2 * i + 1), resident((2 * i, 2 * i + 1), 1 - c)):
+    def resident_other(pair):
+        for r, (value, top, total) in zip(pair, resident(pair, 1 - c)):
             coded, scale = code(value, 1)
             esend[r] = to_code(coded)
             put_columns(estat.at[r], top, total, scale)
-        return carry
-
+            go_pair(e_copies[r])
+
+    e_copies = [
+        (link(esend.at[r], ebuf.at[r], dev_sib), link(estat.at[r], efrom.at[r], dev_sib)) for r in range(NR)
+    ]
     lax.fori_loop(0, 2 * NR, fill, 0)
-    lax.fori_loop(0, 1, resident_other, 0)
+    resident_other(PAIRS[0])
 
     pass_on(2)
     d_p1.wait_recv()
@@ -306,41 +310,32 @@
     d_m0.wait_recv()
     go(share_d[2])
     swap_shared(1)
+    resident_other(PAIRS[1])
+
+    pass_on(3)
     swap_shared(2)
-
-    for slot in (1, 2):
-        share_d[slot].wait_recv()
-        share_s[slot].wait_recv()
-        send_part(slot, jnp.transpose(nt(hid[...], kvt[slot])), m_copies[slot])
-        if slot == 1:
-            pass_on(3)
-
-    def over_lanes(starts, size, at):
-        part = sum(nt(hid[at, start:start + size], kvt[3, :, start:start + size]) for start in starts)
-        return jnp.transpose(part)
-
-    direct_at = ((4 * SHARE, HALF_D // 2 + 4 * SHARE), 2 * DIRECT)
-    shared_at = ((0, HALF_D // 2), 4 * SHARE)
+    share_d[1].wait_recv()
+    share_s[1].wait_recv()
+    send_part(1, nt(kvt[1], hid[...]), m_copies[1])
     df_p.wait_recv()
     df_m.wait_recv()
     go(share_d[3])
     swap_shared(3)
+    share_d[2].wait_recv()
+    share_s[2].wait_recv()
+    send_part(2, nt(kvt[2], hid[...]), m_copies[2])
+
+    def over_lanes(starts, size, at):
+        return sum(nt(kvt[3, :, start:start + size], hid[at, start:start + size]) for start in starts)
+
     share_d[3].wait_recv()
-    lat[origin[3]] = over_lanes(*direct_at, slice(None))
+    lat[origin[3]] = over_lanes((4 * SHARE, HALF_D // 2 + 4 * SHARE), 2 * DIRECT, slice(None))
     share_s[3].wait_recv()
     for i, at in enumerate(tails):
-        send_part(3, lat[origin[3], :, at] + over_lanes(*shared_at, at), m_copies[3 + i], at)
-
-    lax.fori_loop(1, 2, resident_other, 0)
-    e_copies = [
-        (link(esend.at[r], ebuf.at[r], dev_sib), link(estat.at[r], efrom.at[r], dev_sib)) for r in range(NR)
-    ]
-    for pair in e_copies:
-        go_pair(pair)
+        send_part(
+            3, lat[origin[3], :, at] + over_lanes((0, HALF_D // 2), 4 * SHARE, at), m_copies[3 + i], at
+        )
     lax.fori_loop(0, 2, resident_own, 0)
-    for pair in e_copies:
-        wait_pair(pair)
-    lax.fori_loop(0, NR, add_other, 0)
 
     for slot in range(4):
         for pair in m_copies[slot:] if slot == 3 else m_copies[slot:slot + 1]:
@@ -366,30 +361,40 @@
         column = lax.broadcasted_iota(I32, (CAPTOK, KVX), 1)
         return jnp.where((column == KVW) & empty, 1.0, page_rows).astype(BF16)
 
-    half = CAPTOK // 2
-    a_r0 = link(packed.at[2, pl.ds(0, half)], relay.at[0], dev_zp)
-    a_r1 = link(packed.at[2, pl.ds(half, half)], relay.at[1], dev_zm)
-    a_p = link(packed.at[0], arr.at[1, c], dev_zp)
-    a_m = link(packed.at[1], arr.at[2, c], dev_zm)
-    a_f0 = link(relay.at[0], arr.at[3, c, pl.ds(0, half)], dev_zp)
-    a_f1 = link(relay.at[1], arr.at[3, c, pl.ds(half, half)], dev_zm)
-    a_share = [link(arr.at[slot, c], arr.at[slot, c], dev_sib) for slot in range(3)]
-    a_share3 = [
-        link(arr.at[3, c, pl.ds(0, half)], arr.at[3, c, pl.ds(0, half)], dev_sib),
-        link(arr.at[3, c, pl.ds(half, half)], arr.at[3, c, pl.ds(half, half)], dev_sib),
-    ]
+    first, second = pl.ds(0, HALF), pl.ds(HALF, HALF)
+    a_p = [link(packed.at[0, at], arr.at[part, c], dev_zp) for at, part in ((first, 2), (second, 4))]
+    a_m = [link(packed.at[1, at], arr.at[part, c], dev_zm) for at, part in ((first, 3), (second, 5))]
+    a_r0 = link(packed.at[2, first], relay.at[0], dev_zp)
+    a_r1 = link(packed.at[2, second], relay.at[1], dev_zm)
+    a_f0 = link(relay.at[0], arr.at[6, c], dev_zp)
+    a_f1 = link(relay.at[1], arr.at[7, c], dev_zm)
+    a_share = [link(arr.at[part, c], arr.at[part, c], dev_sib) for part in range(8)]
+    packed[0] = pack_for(lax.rem(b + 1, 4))
+    go(a_p[0])
+    packed[1] = pack_for(lax.rem(b + 3, 4))
+    go(a_m[0])
     packed[2] = pack_for(lax.rem(b + 2, 4))
     go(a_r0)
     go(a_r1)
-    packed[0] = pack_for(lax.rem(b + 1, 4))
-    go(a_p)
-    packed[1] = pack_for(lax.rem(b + 3, 4))
-    go(a_m)
-    arr[0, c] = pack_for(b)
+    go(a_p[1])
+    go(a_m[1])
+    own_pages = pack_for(b)
+    arr[0, c] = own_pages[:HALF]
     go(a_share[0])
+    arr[1, c] = own_pages[HALF:]
+    go(a_share[1])
+
+    def swap(copies, parts):
+        for copy, part in zip(copies, parts):
+            copy.wait_recv()
+            go(a_share[part])
+
+    def ready(parts):
+        for part in parts:
+            a_share[part].wait_recv()
 
     def pages_step(pair, first, last):
-        keys = arr[first:last + 1].reshape((last + 1 - first) * 2 * CAPTOK, KVX)
+        keys = arr[first:last + 1].reshape((last + 1 - first) * CAPTOK, KVX)
         scores = [nt(qbuf[c * NR + r], keys) for r in pair]
         weights = []
         for r, score in zip(pair, scores):
@@ -403,34 +408,30 @@
             for r, (w, shrink, top, total) in zip(pair, weights)
         ]
 
-    def pages_of(first, last):
-        def body(i, carry):
-            pair = (2 * i, 2 * i + 1)
-            for r, state in zip(pair, pages_step(pair, first, last)):
-                acc[r], ms[r], ls[r] = state
-            return carry
-
-        lax.fori_loop(0, 2, body, 0)
-
+    def pages_of(pair, first, last):
+        for r, state in zip(pair, pages_step(pair, first, last)):
+            acc[r], ms[r], ls[r] = state
+
+    for pair in e_copies:
+        wait_pair(pair)
+    lax.fori_loop(0, NR, add_other, 0)
+    ready((0, 1))
+    pages_of(PAIRS[0], 0, 1)
+    swap((a_p[0], a_m[0]), (2, 3))
+    pages_of(PAIRS[1], 0, 1)
     a_r0.wait_recv()
     go(a_f0)
     a_r1.wait_recv()
     go(a_f1)
-    a_share[0].wait_recv()
-    pages_of(0, 0)
-    a_p.wait_recv()
-    go(a_share[1])
-    a_m.wait_recv()
-    go(a_share[2])
-    a_share[1].wait_recv()
-    a_share[2].wait_recv()
-    pages_of(1, 2)
-    a_f0.wait_recv()
-    go(a_share3[0])
-    a_f1.wait_recv()
-    go(a_share3[1])
-    a_share3[0].wait_recv()
-    a_share3[1].wait_recv()
+    ready((2, 3))
+    pages_of(PAIRS[0], 2, 3)
+    swap((a_p[1], a_m[1]), (4, 5))
+    pages_of(PAIRS[1], 2, 3)
+    ready((4, 5))
+    pages_of((0,), 4, 5)
+    swap((a_f0, a_f1), (6, 7))
+    pages_of((1,), 4, 5)
+    ready((6, 7))
 
     def merge(parts):
         top = parts[0][1][0]
@@ -478,16 +479,6 @@
         pair[0].start()
         pair[1].start()
 
-    for r in range(NR):
-        value, top, total = pages_step((r,), 3, 3)[0]
-        coded, scale = code(value, 1)
-        osend[r] = to_code(jnp.transpose(coded)).reshape(4, 2, 64, QROWS)
-        stat = jnp.transpose(jnp.where(lane == 0, top * log2_scale + jnp.log(scale) * log2_e, 1.0 / scale))
-        ostat[r, 0] = stat[0:1]
-        ostat[r, 1] = jnp.sum(jnp.transpose(total), axis=0, keepdims=True) * stat[1:2]
-        for k in range(4):
-            start_pair(y_pair(r, k))
-
     def relay_sums(r, carry):
         for k, to in ((0, yp), (1, ym)):
             wait_pair(y_pair(r, k))
@@ -496,6 +487,18 @@
             ]))
             start_pair(y_pair(r, 4 + k))
         return carry
+
+    for r in range(NR):
+        value, top, total = pages_step((r,), 6 if r < 2 else 4, 7)[0]
+        coded, scale = code(value, 1)
+        osend[r] = to_code(jnp.transpose(coded)).reshape(4, 2, 64, QROWS)
+        stat = jnp.transpose(jnp.where(lane == 0, top * log2_scale + jnp.log(scale) * log2_e, 1.0 / scale))
+        ostat[r, 0] = stat[0:1]
+        ostat[r, 1] = jnp.sum(jnp.transpose(total), axis=0, keepdims=True) * stat[1:2]
+        for k in range(4):
+            start_pair(y_pair(r, k))
+        if r >= 2:
+            relay_sums(r - 2, 0)
 
     def sums_over_y(r, carry):
         for k in range(2, 6):
@@ -528,7 +531,8 @@
             pair[1].wait_send()
         return carry
 
-    for stage in (relay_sums, sums_over_y, last_sums, finish):
+    lax.fori_loop(2, NR, relay_sums, 0)
+    for stage in (sums_over_y, last_sums, finish):
         lax.fori_loop(0, NR, stage, 0)
     for copy in started:
         copy.wait_send()
@@ -564,8 +568,8 @@
             pltpu.VMEM((4, 1, TOK), F32),
             pltpu.VMEM((KVX, TOK), BF16),
             pltpu.VMEM((3, CAPTOK, KVX), BF16),
-            pltpu.VMEM((2, CAPTOK // 2, KVX), BF16),
-            pltpu.VMEM((4, 2, CAPTOK, KVX), BF16),
+            pltpu.VMEM((2, HALF, KVX), BF16),
+            pltpu.VMEM((8, 2, HALF, KVX), BF16),
             pltpu.VMEM((1, TOK), I32),
             pltpu.VMEM((2 * NR, 4, 64, KVW), BF16),
             pltpu.VMEM((2 * NR, QROWS, KVX), BF16),

time: 75.4 us -> 69.8 us (0.926)
  Pallas kernels: 73.3 us -> 67.7 us
    pallas_call x1, Pallas kernels: 73.3 us -> 67.7 us  [on_device(): pl.pallas_call(kernel, out_shape=jax.ShapeDtypeStruct((4, 2 * NR, 32, 64)...]
where the time goes in v5:
time: 69.8 us; the launch traced here: 69.5 us
  Pallas kernels  67.7 us (97%)
  local copies, waits for them, and re-layouts  1.87 us (3%)
    pallas_call x1, Pallas kernels, on_device(): pl.pallas_call(kernel, out_shape=jax.ShapeDtypeStruct((4, 2 * NR, 32, 64)...  67.7 us
    unnamed x1, local copies, waits for them, and re-layouts  1.87 us

profile of v5, /device:TPU:1, one launch (start us, length us, event | category | flops | bytes accessed | tf_op | source)
XLA Modules:
  0.0 69.5 jit_solution(3403263114989821990)
XLA Ops:
  0.0 67.7 %shard_map.100 = f32[4,8,32,64]{3,2,1,0:T(8,128)} custom-call(bf16[384,3584]{1,0:T(8,128)(2,1)} %hidden.1, bf16[144,3584]{1,0:T(8,128)(2,1)} %bitcast.7, f32[1,512]{1,0:T(1,128)} %bitcast.8, s32[1,24]{1,0:T(1,128)} %bitcast.9, s32[24]{0:T(128)} %request.1, bf16[4,8,64,576]{3,2,1,0:T(8,128)(2,1)} %queries.1, bf16[8,576,512]{2,1,0:T(8,128)(2,1)} %bitcast.6, ...), custom_call_target="tpu_custom_call" | custom-call | flops 7500000256 | bytes 12000000 | tf_op jit(solution)/shard_map/pallas_call | solution.py:556
  67.7 1.9 %copy.12 = f32[4,8,64,32]{2,3,1,0:T(8,128)} copy(f32[4,8,64,32]{2,3,1,0:T(8,128)} %bitcast.5) | data formatting | bytes 524288

commit v6 on v5

--- a/solution.py
+++ b/solution.py
@@ -44,7 +44,7 @@
     hidden, kv_down, gain, owner, request, queries, cache, lengths, cosine, sine,
     out,
     hid, kvt, lat, mps, mpr, mss, msr, rows, packed, relay, arr, tok,
-    qraw, qbuf, kbuf, esend, estat, ebuf, efrom, acc, ms, ls, osend, ostat, ybuf, ystat, rsend, rstat, mbuf, mstat, fbuf, fstat,
+    vt, qraw, qbuf, kbuf, esend, estat, ebuf, efrom, acc, ms, ls, osend, ostat, ybuf, ystat, rsend, rstat, mbuf, mstat, fbuf, fstat,
     loc, send, recv,
 ):
     s, b, p = lax.axis_index("seq"), lax.axis_index("batch"), lax.axis_index("mp")
@@ -204,14 +204,6 @@
             most = jnp.maximum(most, score[:, j * 128:j * 128 + 128])
         return most
 
-    lane = lax.broadcasted_iota(I32, (QROWS, 128), 1)
-
-    def put_columns(stat_ref, top, total, scale):
-        stat = jnp.transpose(jnp.where(lane == 0, top * log2_scale, scale))
-        stat_ref[0] = stat[0:1]
-        stat_ref[1] = jnp.sum(jnp.transpose(total), axis=0, keepdims=True)
-        stat_ref[2] = stat[1:2]
-
     def resident(pair, half):
         at = lax.broadcasted_iota(I32, (1, CTXD), 1) + s * CTXD
         scores = [
@@ -222,28 +214,27 @@
         for score in scores:
             top = jnp.maximum(jnp.max(peak(score), axis=1, keepdims=True), floor_value)
             w = weigh(score, top)
-            weights.append((w.astype(BF16), jnp.broadcast_to(top, (QROWS, 128)), fold(w)))
+            top = jnp.transpose(jnp.broadcast_to(top, (QROWS, 128)))[0:1]
+            weights.append((w.astype(BF16), top, jnp.sum(jnp.transpose(fold(w)), axis=0, keepdims=True)))
         return [
-            (nt(w, kbuf[half * NR + r, :LATW, :]), top, total) for r, (w, top, total) in zip(pair, weights)
+            (nt(kbuf[half * NR + r, :LATW, :], w), top, total) for r, (w, top, total) in zip(pair, weights)
         ]
 
-    def resident_own(i, carry):
-        for r, state in zip((2 * i, 2 * i + 1), resident((2 * i, 2 * i + 1), c)):
-            acc[r], ms[r], ls[r] = state
-        return carry
-
-    def add_other(r, carry):
-        row = lax.broadcasted_iota(I32, (128, QROWS), 0)
-        stat = jnp.where(row == 0, efrom[r, 0], jnp.where(row == 1, efrom[r, 1], efrom[r, 2]))
-        stat = jnp.transpose(stat)
-        top2, total2, scale2 = stat[:, 0:1] * (1.0 / log2_scale), stat[:, 1:2], stat[:, 2:3]
-        old = ms[r][:, :1]
+    def columns(first, count=1):
+        return slice(first * QROWS, (first + count) * QROWS)
+
+    def resident_own(pair):
+        for r, (value, top, total) in zip(pair, resident(pair, c)):
+            acc[:, columns(r)], ms[:, columns(r)], ls[:, columns(r)] = value, top, total
+
+    def add_other(r):
+        at = columns(r)
+        old, top2 = ms[:, at], efrom[r, 0]
         top = jnp.maximum(old, top2)
         keep, gain2 = jnp.exp2((old - top) * log2_scale), jnp.exp2((top2 - top) * log2_scale)
-        acc[r] = acc[r] * keep + from_code(ebuf[r]) * (gain2 * scale2)
-        ms[r] = jnp.broadcast_to(top, (QROWS, 128))
-        ls[r] = ls[r] * keep + jnp.where(lane == 0, gain2 * total2, 0.0)
-        return carry
+        acc[:, at] = acc[:, at] * keep + from_code(ebuf[r]) * (gain2 * efrom[r, 2])
+        ls[:, at] = ls[:, at] * keep + gain2 * efrom[r, 1]
+        ms[:, at] = top
 
     load_hid.wait()
     load_kv.wait()
@@ -293,9 +284,10 @@
 
     def resident_other(pair):
         for r, (value, top, total) in zip(pair, resident(pair, 1 - c)):
-            coded, scale = code(value, 1)
+            coded, scale = code(value, 0)
             esend[r] = to_code(coded)
-            put_columns(estat.at[r], top, total, scale)
+            for k, row in enumerate((top, total, scale)):
+                estat[r, k] = row
             go_pair(e_copies[r])
 
     e_copies = [
@@ -335,7 +327,8 @@
         send_part(
             3, lat[origin[3], :, at] + over_lanes((0, HALF_D // 2), 4 * SHARE, at), m_copies[3 + i], at
         )
-    lax.fori_loop(0, 2, resident_own, 0)
+    for pair in PAIRS:
+        resident_own(pair)
 
     for slot in range(4):
         for pair in m_copies[slot:] if slot == 3 else m_copies[slot:slot + 1]:
@@ -393,45 +386,51 @@
         for part in parts:
             a_share[part].wait_recv()
 
-    def pages_step(pair, first, last):
-        keys = arr[first:last + 1].reshape((last + 1 - first) * CAPTOK, KVX)
-        scores = [nt(qbuf[c * NR + r], keys) for r in pair]
-        weights = []
-        for r, score in zip(pair, scores):
-            old = ms[r][:, :1]
-            top = jnp.maximum(old, jnp.max(peak(score), axis=1, keepdims=True))
-            shrink = jnp.exp2((old - top) * log2_scale)
-            w = weigh(score, top)
-            weights.append((w.astype(BF16), shrink, top, ls[r] * shrink + fold(w)))
-        return [
-            (acc[r] * shrink + nn(w, keys[:, :LATW]), jnp.broadcast_to(top, (QROWS, 128)), total)
-            for r, (w, shrink, top, total) in zip(pair, weights)
-        ]
-
-    def pages_of(pair, first, last):
-        for r, state in zip(pair, pages_step(pair, first, last)):
-            acc[r], ms[r], ls[r] = state
+    def turn_values(first, last):
+        size = (last + 1 - first) * CAPTOK
+        values = arr[first:last + 1].reshape(size, KVX)[:, :LATW]
+        vt[:, first * CAPTOK:first * CAPTOK + size] = jnp.transpose(values)
+
+    def pages_step(request, count, first, last):
+        size, at = (last + 1 - first) * CAPTOK, columns(request, count)
+        keys = arr[first:last + 1].reshape(size, KVX)
+        score = nt(keys, qbuf[pl.ds(c * NR + request, count)].reshape(count * QROWS, KVX))
+        old = ms[:, at]
+        top = jnp.maximum(old, jnp.max(score, axis=0, keepdims=True))
+        shrink = jnp.exp2((old - top) * log2_scale)
+        w = weigh(score, top)
+        total = ls[:, at] * shrink + jnp.sum(w, axis=0, keepdims=True)
+        value = acc[:, at] * shrink + nn(vt[:, first * CAPTOK:first * CAPTOK + size], w.astype(BF16))
+        return value, top, total
+
+    def pages_of(request, count, first, last):
+        at = columns(request, count)
+        acc[:, at], ms[:, at], ls[:, at] = pages_step(request, count, first, last)
 
     for pair in e_copies:
         wait_pair(pair)
-    lax.fori_loop(0, NR, add_other, 0)
+    for r in range(NR):
+        add_other(r)
     ready((0, 1))
-    pages_of(PAIRS[0], 0, 1)
+    turn_values(0, 1)
+    pages_of(0, 2, 0, 1)
     swap((a_p[0], a_m[0]), (2, 3))
-    pages_of(PAIRS[1], 0, 1)
+    pages_of(2, 2, 0, 1)
     a_r0.wait_recv()
     go(a_f0)
     a_r1.wait_recv()
     go(a_f1)
     ready((2, 3))
-    pages_of(PAIRS[0], 2, 3)
+    turn_values(2, 3)
+    pages_of(0, 2, 2, 3)
     swap((a_p[1], a_m[1]), (4, 5))
-    pages_of(PAIRS[1], 2, 3)
+    pages_of(2, 2, 2, 3)
     ready((4, 5))
-    pages_of((0,), 4, 5)
+    turn_values(4, 5)
     swap((a_f0, a_f1), (6, 7))
-    pages_of((1,), 4, 5)
+    pages_of(0, 2, 4, 5)
     ready((6, 7))
+    turn_values(6, 7)
 
     def merge(parts):
         top = parts[0][1][0]
@@ -488,17 +487,17 @@
             start_pair(y_pair(r, 4 + k))
         return carry
 
-    for r in range(NR):
-        value, top, total = pages_step((r,), 6 if r < 2 else 4, 7)[0]
-        coded, scale = code(value, 1)
-        osend[r] = to_code(jnp.transpose(coded)).reshape(4, 2, 64, QROWS)
-        stat = jnp.transpose(jnp.where(lane == 0, top * log2_scale + jnp.log(scale) * log2_e, 1.0 / scale))
-        ostat[r, 0] = stat[0:1]
-        ostat[r, 1] = jnp.sum(jnp.transpose(total), axis=0, keepdims=True) * stat[1:2]
-        for k in range(4):
-            start_pair(y_pair(r, k))
-        if r >= 2:
-            relay_sums(r - 2, 0)
+    for request, first in ((0, 6), (2, 4)):
+        value, top, total = pages_step(request, 2, first, 7)
+        coded, scale = code(value, 0)
+        coded, top, total = to_code(coded), top * log2_scale + jnp.log(scale) * log2_e, total / scale
+        for r in (request, request + 1):
+            at = columns(r - request)
+            osend[r] = coded[:, at].reshape(4, 2, 64, QROWS)
+            ostat[r, 0] = top[:, at]
+            ostat[r, 1] = total[:, at]
+            for k in range(4):
+                start_pair(y_pair(r, k))
 
     def sums_over_y(r, carry):
         for k in range(2, 6):
@@ -531,7 +530,7 @@
             pair[1].wait_send()
         return carry
 
-    lax.fori_loop(2, NR, relay_sums, 0)
+    lax.fori_loop(0, NR, relay_sums, 0)
     for stage in (sums_over_y, last_sums, finish):
         lax.fori_loop(0, NR, stage, 0)
     for copy in started:
@@ -571,16 +570,17 @@
             pltpu.VMEM((2, HALF, KVX), BF16),
             pltpu.VMEM((8, 2, HALF, KVX), BF16),
             pltpu.VMEM((1, TOK), I32),
+            pltpu.VMEM((LATW, 8 * CAPTOK), BF16),
             pltpu.VMEM((2 * NR, 4, 64, KVW), BF16),
             pltpu.VMEM((2 * NR, QROWS, KVX), BF16),
             pltpu.VMEM((2 * NR, KVW, CTXD), BF16),
-            pltpu.VMEM((NR, QROWS, LATW), I16),
+            pltpu.VMEM((NR, LATW, QROWS), I16),
             pltpu.VMEM((NR, 3, 1, QROWS), F32),
-            pltpu.VMEM((NR, QROWS, LATW), I16),
+            pltpu.VMEM((NR, LATW, QROWS), I16),
             pltpu.VMEM((NR, 3, 1, QROWS), F32),
-            pltpu.VMEM((NR, QROWS, LATW), F32),
-            pltpu.VMEM((NR, QROWS, 128), F32),
-            pltpu.VMEM((NR, QROWS, 128), F32),
+            pltpu.VMEM((LATW, NR * QROWS), F32),
+            pltpu.VMEM((1, NR * QROWS), F32),
+            pltpu.VMEM((1, NR * QROWS), F32),
             pltpu.VMEM((NR, 4, 2, 64, QROWS), I16),
             pltpu.VMEM((NR, 2, 1, QROWS), F32),
             pltpu.VMEM((NR, 6, 64, QROWS), I16),

time: 69.8 us -> 70 us (level)
  no operation moved by 1% of the time
where the time goes in v6:
time: 70 us; the launch traced here: 69.8 us
  Pallas kernels  67.9 us (97%)
  local copies, waits for them, and re-layouts  1.87 us (3%)
    pallas_call x1, Pallas kernels, on_device(): pl.pallas_call(kernel, out_shape=jax.ShapeDtypeStruct((4, 2 * NR, 32, 64)...  67.9 us
    unnamed x1, local copies, waits for them, and re-layouts  1.87 us

profile of v6, /device:TPU:1, one launch (start us, length us, event | category | flops | bytes accessed | tf_op | source)
XLA Modules:
  0.0 69.8 jit_solution(2470191408226671269)
XLA Ops:
  0.0 67.9 %shard_map.100 = f32[4,8,32,64]{3,2,1,0:T(8,128)} custom-call(bf16[384,3584]{1,0:T(8,128)(2,1)} %hidden.1, bf16[144,3584]{1,0:T(8,128)(2,1)} %bitcast.7, f32[1,512]{1,0:T(1,128)} %bitcast.8, s32[1,24]{1,0:T(1,128)} %bitcast.9, s32[24]{0:T(128)} %request.1, bf16[4,8,64,576]{3,2,1,0:T(8,128)(2,1)} %queries.1, bf16[8,576,512]{2,1,0:T(8,128)(2,1)} %bitcast.6, ...), custom_call_target="tpu_custom_call" | custom-call | flops 7500000256 | bytes 12000000 | tf_op jit(solution)/shard_map/pallas_call | solution.py:555
  67.9 1.9 %copy.12 = f32[4,8,64,32]{2,3,1,0:T(8,128)} copy(f32[4,8,64,32]{2,3,1,0:T(8,128)} %bitcast.5) | data formatting | bytes 524288

commit v7 on v6

--- a/solution.py
+++ b/solution.py
@@ -41,8 +41,9 @@
 
 
 def kernel(
-    hidden, kv_down, gain, owner, request, queries, cache, lengths, cosine, sine,
-    out,
+    hidden, kv_down, gain_in, owner_in, request_in, queries, cache, lengths_in, cosine_in, sine_in,
+    out_hbm,
+    gain, owner, request, lengths, cosine, sine, out,
     hid, kvt, lat, mps, mpr, mss, msr, rows, packed, relay, arr, tok,
     vt, qraw, qbuf, kbuf, esend, estat, ebuf, efrom, acc, ms, ls, osend, ostat, ybuf, ystat, rsend, rstat, mbuf, mstat, fbuf, fstat,
     loc, send, recv,
@@ -99,20 +100,23 @@
         pair[0].wait_recv()
         pair[1].wait_recv()
 
-    load_kv = pltpu.make_async_copy(kv_down, kvt.at[0], loc.at[0])
-    load_kv.start()
-    load_hid = pltpu.make_async_copy(hidden, hid, loc.at[1])
-    load_hid.start()
-    load_q = []
-    for step in range(4):
-        load_q.append(pltpu.make_async_copy(queries.at[step], qraw.at[:, step], loc.at[2 + step]))
-        load_q[-1].start()
-    load_cache = pltpu.make_async_copy(cache, kbuf, loc.at[6])
-    load_cache.start()
-
     barrier = pltpu.get_barrier_semaphore()
     for dev in (dev_zp, dev_zm, dev_zz, dev_mp, dev_sib, dev_yp, dev_ym, dev_x, dev_x_sib):
         pl.semaphore_signal(barrier, inc=1, device_id=dev, device_id_type=MESH)
+
+    small = [
+        pltpu.make_async_copy(src, dst, loc.at[7 + i])
+        for i, (src, dst) in enumerate((
+            (owner_in, owner), (request_in, request), (lengths_in, lengths), (gain_in, gain), (cosine_in, cosine),
+            (sine_in, sine),
+        ))
+    ]
+    load_kv = pltpu.make_async_copy(kv_down, kvt.at[0], loc.at[0])
+    load_hid = pltpu.make_async_copy(hidden, hid, loc.at[1])
+    load_q = [pltpu.make_async_copy(queries.at[step], qraw.at[:, step], loc.at[2 + step]) for step in range(4)]
+    load_cache = pltpu.make_async_copy(cache, kbuf, loc.at[6])
+    for copy in [load_hid, load_kv] + small:
+        copy.start()
 
     pl.semaphore_wait(barrier, 9)
 
@@ -137,6 +141,8 @@
     d_p1, d_m0 = first_link(1, high, dev_zp), first_link(2, low, dev_zm)
     for copy in (s_p, s_m, d_p0, d_m1):
         go(copy)
+    for copy in load_q + [load_cache]:
+        copy.start()
     sf_p, sf_m = (
         kv_link(1, 3, part_of(0, 0, SHARE // 2), dev_zp),
         kv_link(2, 3, part_of(0, SHARE // 2, SHARE // 2), dev_zm),
@@ -154,23 +160,6 @@
     share_s = [None] + [kv_link(slot, slot, lanes(0, 4 * SHARE), dev_sib) for slot in (1, 2, 3)]
     share_d = [None] + [kv_link(slot, slot, lanes(4 * SHARE, 2 * DIRECT), dev_sib) for slot in (1, 2, 3)]
 
-    token = lax.broadcasted_iota(I32, (1, TOK), 1)
-    token_page = lax.shift_right_logical(token, 4)
-    dest = jnp.zeros((1, TOK), I32)
-    asked = jnp.zeros((1, TOK), I32)
-    counts = [jnp.int32(0)] * 4
-    for page in range(PAGES):
-        to = owner[0, page]
-        rank = jnp.where(to == 0, counts[0], jnp.where(to == 1, counts[1], jnp.where(to == 2, counts[2], counts[3])))
-        counts = [counts[o] + (to == o).astype(I32) for o in range(4)]
-        dest = jnp.where(token_page == page, (to * CAP + rank) * PAGE, dest)
-        asked = jnp.where(token_page == page, request[page] + 1, asked)
-    dest = dest + lax.bitwise_and(token, 15)
-    tok[...] = dest
-
-    label_row = lax.broadcasted_iota(I32, (LABELS, TOK), 0)
-    rows[KVW:, :] = (label_row == asked).astype(F32).astype(BF16)
-
     origin = [lax.rem(b + ahead, 4) for ahead in (0, 3, 1, 2)]
     m_copies = [
         (link(mps.at[slot], mpr.at[slot], dev_mp), link(mss.at[slot], msr.at[slot], dev_mp)) for slot in range(3)
@@ -238,6 +227,7 @@
 
     load_hid.wait()
     load_kv.wait()
+    send_part(0, nt(kvt[0], hid[...]), m_copies[0])
     s_p.wait_recv()
     go(sf_p)
     go(near_p[1])
@@ -248,7 +238,25 @@
     go(near_m[2])
     go(d_p1)
     go(d_m0)
-    send_part(0, nt(kvt[0], hid[...]), m_copies[0])
+
+    for copy in small:
+        copy.wait()
+    token = lax.broadcasted_iota(I32, (1, TOK), 1)
+    token_page = lax.shift_right_logical(token, 4)
+    dest = jnp.zeros((1, TOK), I32)
+    asked = jnp.zeros((1, TOK), I32)
+    counts = [jnp.int32(0)] * 4
+    for page in range(PAGES):
+        to = owner[0, page]
+        rank = jnp.where(to == 0, counts[0], jnp.where(to == 1, counts[1], jnp.where(to == 2, counts[2], counts[3])))
+        counts = [counts[o] + (to == o).astype(I32) for o in range(4)]
+        dest = jnp.where(token_page == page, (to * CAP + rank) * PAGE, dest)
+        asked = jnp.where(token_page == page, request[page] + 1, asked)
+    dest = dest + lax.bitwise_and(token, 15)
+    tok[...] = dest
+
+    label_row = lax.broadcasted_iota(I32, (LABELS, TOK), 0)
+    rows[KVW:, :] = (label_row == asked).astype(F32).astype(BF16)
 
     d_p0.wait_recv()
     go(df_p)
@@ -487,12 +495,12 @@
             start_pair(y_pair(r, 4 + k))
         return carry
 
-    for request, first in ((0, 6), (2, 4)):
-        value, top, total = pages_step(request, 2, first, 7)
+    for first_request, count, first in ((0, 1, 6), (1, 1, 6), (2, 2, 4)):
+        value, top, total = pages_step(first_request, count, first, 7)
         coded, scale = code(value, 0)
         coded, top, total = to_code(coded), top * log2_scale + jnp.log(scale) * log2_e, total / scale
-        for r in (request, request + 1):
-            at = columns(r - request)
+        for r in range(first_request, first_request + count):
+            at = columns(r - first_request)
             osend[r] = coded[:, at].reshape(4, 2, 64, QROWS)
             ostat[r, 0] = top[:, at]
             ostat[r, 1] = total[:, at]
@@ -510,18 +518,22 @@
             start_pair(last_pair(r, k))
         return carry
 
+    def out_copy(wanted):
+        return pltpu.make_async_copy(out.at[:, wanted], out_hbm.at[:, wanted], loc.at[13 + wanted])
+
     def last_sums(r, carry):
         for k in range(3):
             wait_pair(last_pair(r, k))
         own, other = c * NR + r, (1 - c) * NR + r
-        for request, parts in (
+        for wanted, parts in (
             (own, [(mbuf[r, xh, c], mstat[r, xh]), (fbuf[r, 0], fstat[r, 0])]),
             (other, [(fbuf[r, 2], fstat[r, 2]), (fbuf[r, 1], fstat[r, 1])]),
         ):
             value, _, total = merge(parts)
             value = value / total
             for step in range(4):
-                out[step, request] = value[:, 64 * step:64 * step + 64]
+                out[step, wanted] = value[:, 64 * step:64 * step + 64]
+            out_copy(wanted).start()
         return carry
 
     def finish(r, carry):
@@ -533,6 +545,8 @@
     lax.fori_loop(0, NR, relay_sums, 0)
     for stage in (sums_over_y, last_sums, finish):
         lax.fori_loop(0, NR, stage, 0)
+    for wanted in range(2 * NR):
+        out_copy(wanted).wait()
     for copy in started:
         copy.wait_send()
 
@@ -550,14 +564,19 @@
 def on_device(hidden, kv_down, kv_gain, page_owner, page_request, queries, cache, lengths):
     cosine, sine = tables()
     anywhere = pl.BlockSpec(memory_space=pl.ANY)
-    vmem = pl.BlockSpec(memory_space=pltpu.VMEM)
-    smem = pl.BlockSpec(memory_space=pltpu.SMEM)
     sums = pl.pallas_call(
         kernel,
         out_shape=jax.ShapeDtypeStruct((4, 2 * NR, 32, 64), F32),
-        in_specs=[anywhere, anywhere, vmem, smem, smem, anywhere, anywhere, smem, vmem, vmem],
-        out_specs=vmem,
+        in_specs=[anywhere] * 10,
+        out_specs=anywhere,
         scratch_shapes=[
+            pltpu.VMEM((1, LATW), F32),
+            pltpu.SMEM((1, PAGES), I32),
+            pltpu.SMEM((PAGES,), I32),
+            pltpu.SMEM((2 * NR,), I32),
+            pltpu.VMEM((ROPEW // 2, TOK), F32),
+            pltpu.VMEM((ROPEW // 2, TOK), F32),
+            pltpu.VMEM((4, 2 * NR, 32, 64), F32),
             pltpu.VMEM((TOK, HALF_D), BF16),
             pltpu.VMEM((4, BLK, HALF_D), BF16),
             pltpu.VMEM((4, BLK, TOK), F32),
@@ -591,7 +610,7 @@
             pltpu.VMEM((NR, 2, 2, 1, QROWS), F32),
             pltpu.VMEM((NR, 3, 32, QROWS), I16),
             pltpu.VMEM((NR, 3, 2, 1, QROWS), F32),
-            pltpu.SemaphoreType.DMA((7,)),
+            pltpu.SemaphoreType.DMA((13 + 2 * NR,)),
             pltpu.SemaphoreType.DMA((LINKS,)),
             pltpu.SemaphoreType.DMA((LINKS,)),
         ],

time: 70 us -> 68.9 us (0.984)
  Pallas kernels: 67.9 us -> 66.9 us
    pallas_call x1, Pallas kernels: 67.9 us -> 66.9 us  [on_device(): pl.pallas_call(kernel, out_shape=jax.ShapeDtypeStruct((4, 2 * NR, 32, 64)...]
where the time goes in v7:
time: 68.9 us; the launch traced here: 68.8 us
  Pallas kernels  66.9 us (97%)
  local copies, waits for them, and re-layouts  1.87 us (3%)
    pallas_call x1, Pallas kernels, on_device(): pl.pallas_call(kernel, out_shape=jax.ShapeDtypeStruct((4, 2 * NR, 32, 64)...  66.9 us
    unnamed x1, local copies, waits for them, and re-layouts  1.87 us

profile of v7, /device:TPU:1, one launch (start us, length us, event | category | flops | bytes accessed | tf_op | source)
XLA Modules:
  0.0 68.8 jit_solution(14661371728947326304)
XLA Ops:
  0.0 66.9 %shard_map.100 = f32[4,8,32,64]{3,2,1,0:T(8,128)} custom-call(bf16[384,3584]{1,0:T(8,128)(2,1)} %hidden.1, bf16[144,3584]{1,0:T(8,128)(2,1)} %bitcast.7, f32[1,512]{1,0:T(1,128)} %bitcast.8, s32[1,24]{1,0:T(1,128)} %bitcast.9, s32[24]{0:T(128)} %request_in.1, bf16[4,8,64,576]{3,2,1,0:T(8,128)(2,1)} %queries.1, bf16[8,576,512]{2,1,0:T(8,128)(2,1)} %bitcast.6, ...), custom_call_target="tpu_custom_call" | custom-call | flops 7500000256 | bytes 12000000 | tf_op jit(solution)/shard_map/pallas_call | solution.py:567
  66.9 1.9 %copy.12 = f32[4,8,64,32]{2,3,1,0:T(8,128)} copy(f32[4,8,64,32]{2,3,1,0:T(8,128)} %bitcast.5) | data formatting | bytes 524288

commit v8 on v7

--- a/solution.py
+++ b/solution.py
@@ -363,22 +363,25 @@
         return jnp.where((column == KVW) & empty, 1.0, page_rows).astype(BF16)
 
     first, second = pl.ds(0, HALF), pl.ds(HALF, HALF)
-    a_p = [link(packed.at[0, at], arr.at[part, c], dev_zp) for at, part in ((first, 2), (second, 4))]
-    a_m = [link(packed.at[1, at], arr.at[part, c], dev_zm) for at, part in ((first, 3), (second, 5))]
+    mine_at = pl.ds(p * HALF, HALF)
+    here, there = 2 + 2 * p, 4 - 2 * p
+    a_p = link(packed.at[0, mine_at], arr.at[here, c], dev_zp)
+    a_m = link(packed.at[1, mine_at], arr.at[here + 1, c], dev_zm)
+    a_x = [link(arr.at[here + i, c], arr.at[here + i, c], dev_mp) for i in range(2)]
     a_r0 = link(packed.at[2, first], relay.at[0], dev_zp)
     a_r1 = link(packed.at[2, second], relay.at[1], dev_zm)
     a_f0 = link(relay.at[0], arr.at[6, c], dev_zp)
     a_f1 = link(relay.at[1], arr.at[7, c], dev_zm)
-    a_share = [link(arr.at[part, c], arr.at[part, c], dev_sib) for part in range(8)]
+    a_share = [
+        link(arr.at[part, c], arr.at[part, c], dev_sib) for part in (0, 1, here, here + 1, there, there + 1, 6, 7)
+    ]
     packed[0] = pack_for(lax.rem(b + 1, 4))
-    go(a_p[0])
+    go(a_p)
     packed[1] = pack_for(lax.rem(b + 3, 4))
-    go(a_m[0])
+    go(a_m)
     packed[2] = pack_for(lax.rem(b + 2, 4))
     go(a_r0)
     go(a_r1)
-    go(a_p[1])
-    go(a_m[1])
     own_pages = pack_for(b)
     arr[0, c] = own_pages[:HALF]
     go(a_share[0])
@@ -394,51 +397,60 @@
         for part in parts:
             a_share[part].wait_recv()
 
-    def turn_values(first, last):
-        size = (last + 1 - first) * CAPTOK
-        values = arr[first:last + 1].reshape(size, KVX)[:, :LATW]
-        vt[:, first * CAPTOK:first * CAPTOK + size] = jnp.transpose(values)
-
-    def pages_step(request, count, first, last):
-        size, at = (last + 1 - first) * CAPTOK, columns(request, count)
-        keys = arr[first:last + 1].reshape(size, KVX)
-        score = nt(keys, qbuf[pl.ds(c * NR + request, count)].reshape(count * QROWS, KVX))
+    starts = (0, here, there, 6)
+
+    def turn_values(group):
+        size = 2 * CAPTOK
+        values = arr[pl.ds(starts[group], 2)].reshape(size, KVX)[:, :LATW]
+        vt[:, group * size:(group + 1) * size] = jnp.transpose(values)
+
+    def pages_step(request, count, group, groups=1):
+        size, at = 2 * CAPTOK, columns(request, count)
+        q = qbuf[pl.ds(c * NR + request, count)].reshape(count * QROWS, KVX)
+        score = jnp.concatenate([
+            nt(arr[pl.ds(starts[g], 2)].reshape(size, KVX), q) for g in range(group, group + groups)
+        ])
         old = ms[:, at]
         top = jnp.maximum(old, jnp.max(score, axis=0, keepdims=True))
         shrink = jnp.exp2((old - top) * log2_scale)
         w = weigh(score, top)
         total = ls[:, at] * shrink + jnp.sum(w, axis=0, keepdims=True)
-        value = acc[:, at] * shrink + nn(vt[:, first * CAPTOK:first * CAPTOK + size], w.astype(BF16))
+        value = acc[:, at] * shrink + nn(vt[:, group * size:(group + groups) * size], w.astype(BF16))
         return value, top, total
 
-    def pages_of(request, count, first, last):
+    def pages_of(request, count, group):
         at = columns(request, count)
-        acc[:, at], ms[:, at], ls[:, at] = pages_step(request, count, first, last)
+        acc[:, at], ms[:, at], ls[:, at] = pages_step(request, count, group)
 
     for pair in e_copies:
         wait_pair(pair)
     for r in range(NR):
         add_other(r)
     ready((0, 1))
-    turn_values(0, 1)
-    pages_of(0, 2, 0, 1)
-    swap((a_p[0], a_m[0]), (2, 3))
-    pages_of(2, 2, 0, 1)
+    turn_values(0)
+    pages_of(0, 2, 0)
+    a_p.wait_recv()
+    go(a_x[0])
+    go(a_share[2])
+    a_m.wait_recv()
+    go(a_x[1])
+    go(a_share[3])
+    pages_of(2, 2, 0)
     a_r0.wait_recv()
     go(a_f0)
     a_r1.wait_recv()
     go(a_f1)
     ready((2, 3))
-    turn_values(2, 3)
-    pages_of(0, 2, 2, 3)
-    swap((a_p[1], a_m[1]), (4, 5))
-    pages_of(2, 2, 2, 3)
+    turn_values(1)
+    pages_of(0, 2, 1)
+    swap(a_x, (4, 5))
+    pages_of(2, 2, 1)
+    swap((a_f0, a_f1), (6, 7))
     ready((4, 5))
-    turn_values(4, 5)
-    swap((a_f0, a_f1), (6, 7))
-    pages_of(0, 2, 4, 5)
+    turn_values(2)
+    pages_of(0, 2, 2)
     ready((6, 7))
-    turn_values(6, 7)
+    turn_values(3)
 
     def merge(parts):
         top = parts[0][1][0]
@@ -495,17 +507,16 @@
             start_pair(y_pair(r, 4 + k))
         return carry
 
-    for first_request, count, first in ((0, 1, 6), (1, 1, 6), (2, 2, 4)):
-        value, top, total = pages_step(first_request, count, first, 7)
+    for r in range(NR):
+        value, top, total = pages_step(r, 1, 3) if r < 2 else pages_step(r, 1, 2, 2)
         coded, scale = code(value, 0)
-        coded, top, total = to_code(coded), top * log2_scale + jnp.log(scale) * log2_e, total / scale
-        for r in range(first_request, first_request + count):
-            at = columns(r - first_request)
-            osend[r] = coded[:, at].reshape(4, 2, 64, QROWS)
-            ostat[r, 0] = top[:, at]
-            ostat[r, 1] = total[:, at]
-            for k in range(4):
-                start_pair(y_pair(r, k))
+        osend[r] = to_code(coded).reshape(4, 2, 64, QROWS)
+        ostat[r, 0] = top * log2_scale + jnp.log(scale) * log2_e
+        ostat[r, 1] = total / scale
+        for k in range(4):
+            start_pair(y_pair(r, k))
+        if r == 2:
+            lax.fori_loop(0, 2, relay_sums, 0)
 
     def sums_over_y(r, carry):
         for k in range(2, 6):
@@ -542,7 +553,7 @@
             pair[1].wait_send()
         return carry
 
-    lax.fori_loop(0, NR, relay_sums, 0)
+    lax.fori_loop(2, NR, relay_sums, 0)
     for stage in (sums_over_y, last_sums, finish):
         lax.fori_loop(0, NR, stage, 0)
     for wanted in range(2 * NR):

time: 68.9 us -> 69.4 us (level)
  no operation moved by 1% of the time
where the time goes in v8:
time: 69.4 us; the launch traced here: 69.3 us
  Pallas kernels  67.4 us (97%)
  local copies, waits for them, and re-layouts  1.87 us (3%)
    pallas_call x1, Pallas kernels, on_device(): pl.pallas_call(kernel, out_shape=jax.ShapeDtypeStruct((4, 2 * NR, 32, 64)...  67.4 us
    unnamed x1, local copies, waits for them, and re-layouts  1.87 us

profile of v8, /device:TPU:1, one launch (start us, length us, event | category | flops | bytes accessed | tf_op | source)
XLA Modules:
  0.0 69.3 jit_solution(5307025636815386995)
XLA Ops:
  0.0 67.4 %shard_map.100 = f32[4,8,32,64]{3,2,1,0:T(8,128)} custom-call(bf16[384,3584]{1,0:T(8,128)(2,1)} %hidden.1, bf16[144,3584]{1,0:T(8,128)(2,1)} %bitcast.7, f32[1,512]{1,0:T(1,128)} %bitcast.8, s32[1,24]{1,0:T(1,128)} %bitcast.9, s32[24]{0:T(128)} %request_in.1, bf16[4,8,64,576]{3,2,1,0:T(8,128)(2,1)} %queries.1, bf16[8,576,512]{2,1,0:T(8,128)(2,1)} %bitcast.6, ...), custom_call_target="tpu_custom_call" | custom-call | flops 7500000256 | bytes 12000000 | tf_op jit(solution)/shard_map/pallas_call | solution.py:578
  67.4 1.9 %copy.12 = f32[4,8,64,32]{2,3,1,0:T(8,128)} copy(f32[4,8,64,32]{2,3,1,0:T(8,128)} %bitcast.5) | data formatting | bytes 524288

commit v9 on v7

--- a/solution.py
+++ b/solution.py
@@ -19,6 +19,7 @@
 code_top = 32767.0
 
 TOK, HALF_D, KVW, LATW, ROPEW = 384, 3584, 576, 512, 64
+USED = 16
 LABELS = 64
 KVX = KVW + LABELS
 BLK = 144
@@ -29,7 +30,6 @@
 QROWS = 256
 CTXD = 512
 NR = 4
-PAIRS = ((0, 1), (2, 3))
 
 
 def nt(a, b):
@@ -45,7 +45,7 @@
     out_hbm,
     gain, owner, request, lengths, cosine, sine, out,
     hid, kvt, lat, mps, mpr, mss, msr, rows, packed, relay, arr, tok,
-    vt, qraw, qbuf, kbuf, esend, estat, ebuf, efrom, acc, ms, ls, osend, ostat, ybuf, ystat, rsend, rstat, mbuf, mstat, fbuf, fstat,
+    vt, qraw, qbuf, kbuf, acc, ms, ls, osend, ostat, ybuf, ystat, rsend, rstat, mbuf, mstat, fbuf, fstat,
     loc, send, recv,
 ):
     s, b, p = lax.axis_index("seq"), lax.axis_index("batch"), lax.axis_index("mp")
@@ -113,8 +113,8 @@
     ]
     load_kv = pltpu.make_async_copy(kv_down, kvt.at[0], loc.at[0])
     load_hid = pltpu.make_async_copy(hidden, hid, loc.at[1])
-    load_q = [pltpu.make_async_copy(queries.at[step], qraw.at[:, step], loc.at[2 + step]) for step in range(4)]
-    load_cache = pltpu.make_async_copy(cache, kbuf, loc.at[6])
+    load_q = [pltpu.make_async_copy(queries.at[step, pl.ds(c * NR, NR)], qraw.at[:, step], loc.at[2 + step]) for step in range(4)]
+    load_cache = pltpu.make_async_copy(cache.at[pl.ds(c * NR, NR)], kbuf.at[0], loc.at[6])
     for copy in [load_hid, load_kv] + small:
         copy.start()
 
@@ -143,6 +143,8 @@
         go(copy)
     for copy in load_q + [load_cache]:
         copy.start()
+    cache_out = link(cache.at[pl.ds((1 - c) * NR, NR)], kbuf.at[1], dev_sib)
+    go(cache_out)
     sf_p, sf_m = (
         kv_link(1, 3, part_of(0, 0, SHARE // 2), dev_zp),
         kv_link(2, 3, part_of(0, SHARE // 2, SHARE // 2), dev_zm),
@@ -193,37 +195,28 @@
             most = jnp.maximum(most, score[:, j * 128:j * 128 + 128])
         return most
 
-    def resident(pair, half):
-        at = lax.broadcasted_iota(I32, (1, CTXD), 1) + s * CTXD
+    def columns(first, count=1):
+        return slice(first * QROWS, (first + count) * QROWS)
+
+    def resident(requests):
+        at = lax.broadcasted_iota(I32, (1, CTXD), 1)
         scores = [
-            jnp.where(at < lengths[half * NR + r], nn(qbuf[half * NR + r, :, :KVW], kbuf[half * NR + r]), masked_value)
-            for r in pair
+            [
+                jnp.where(at + place * CTXD < lengths[c * NR + r], nn(qbuf[r, :, :KVW], kbuf[part, r]), masked_value)
+                for part, place in enumerate((s, sib))
+            ]
+            for r in requests
         ]
         weights = []
-        for score in scores:
-            top = jnp.maximum(jnp.max(peak(score), axis=1, keepdims=True), floor_value)
-            w = weigh(score, top)
-            top = jnp.transpose(jnp.broadcast_to(top, (QROWS, 128)))[0:1]
-            weights.append((w.astype(BF16), top, jnp.sum(jnp.transpose(fold(w)), axis=0, keepdims=True)))
-        return [
-            (nt(kbuf[half * NR + r, :LATW, :], w), top, total) for r, (w, top, total) in zip(pair, weights)
-        ]
-
-    def columns(first, count=1):
-        return slice(first * QROWS, (first + count) * QROWS)
-
-    def resident_own(pair):
-        for r, (value, top, total) in zip(pair, resident(pair, c)):
-            acc[:, columns(r)], ms[:, columns(r)], ls[:, columns(r)] = value, top, total
-
-    def add_other(r):
-        at = columns(r)
-        old, top2 = ms[:, at], efrom[r, 0]
-        top = jnp.maximum(old, top2)
-        keep, gain2 = jnp.exp2((old - top) * log2_scale), jnp.exp2((top2 - top) * log2_scale)
-        acc[:, at] = acc[:, at] * keep + from_code(ebuf[r]) * (gain2 * efrom[r, 2])
-        ls[:, at] = ls[:, at] * keep + gain2 * efrom[r, 1]
-        ms[:, at] = top
+        for r, (score0, score1) in zip(requests, scores):
+            top = jnp.max(jnp.maximum(peak(score0), peak(score1)), axis=1, keepdims=True)
+            top = jnp.maximum(top, floor_value)
+            w0, w1 = weigh(score0, top), weigh(score1, top)
+            ms[:, columns(r)] = jnp.transpose(jnp.broadcast_to(top, (QROWS, 128)))[0:1]
+            ls[:, columns(r)] = jnp.sum(jnp.transpose(fold(w0) + fold(w1)), axis=0, keepdims=True)
+            weights.append((w0.astype(BF16), w1.astype(BF16)))
+        for r, (w0, w1) in zip(requests, weights):
+            acc[:, columns(r)] = nt(kbuf[0, r, :LATW, :], w0) + nt(kbuf[1, r, :LATW, :], w1)
 
     load_hid.wait()
     load_kv.wait()
@@ -256,7 +249,7 @@
     tok[...] = dest
 
     label_row = lax.broadcasted_iota(I32, (LABELS, TOK), 0)
-    rows[KVW:, :] = (label_row == asked).astype(F32).astype(BF16)
+    rows[KVW:, :] = ((label_row == asked) | (label_row == USED)).astype(F32).astype(BF16)
 
     d_p0.wait_recv()
     go(df_p)
@@ -287,22 +280,13 @@
 
     def fill(r, carry):
         qbuf[r, :, :KVW] = qraw[r].reshape(QROWS, KVW)
-        qbuf[r, :, KVW:] = jnp.where(label_at == r + 1, 0.0, masked_value).astype(BF16)
+        opened = (label_at == c * NR + r + 1) | (label_at == USED)
+        qbuf[r, :, KVW:] = jnp.where(opened, 0.0, masked_value).astype(BF16)
         return carry
 
-    def resident_other(pair):
-        for r, (value, top, total) in zip(pair, resident(pair, 1 - c)):
-            coded, scale = code(value, 0)
-            esend[r] = to_code(coded)
-            for k, row in enumerate((top, total, scale)):
-                estat[r, k] = row
-            go_pair(e_copies[r])
-
-    e_copies = [
-        (link(esend.at[r], ebuf.at[r], dev_sib), link(estat.at[r], efrom.at[r], dev_sib)) for r in range(NR)
-    ]
-    lax.fori_loop(0, 2 * NR, fill, 0)
-    resident_other(PAIRS[0])
+    lax.fori_loop(0, NR, fill, 0)
+    cache_out.wait_recv()
+    resident((0,))
 
     pass_on(2)
     d_p1.wait_recv()
@@ -310,7 +294,7 @@
     d_m0.wait_recv()
     go(share_d[2])
     swap_shared(1)
-    resident_other(PAIRS[1])
+    resident((1,))
 
     pass_on(3)
     swap_shared(2)
@@ -335,8 +319,7 @@
         send_part(
             3, lat[origin[3], :, at] + over_lanes((0, HALF_D // 2), 4 * SHARE, at), m_copies[3 + i], at
         )
-    for pair in PAIRS:
-        resident_own(pair)
+    resident((2, 3))
 
     for slot in range(4):
         for pair in m_copies[slot:] if slot == 3 else m_copies[slot:slot + 1]:
@@ -356,9 +339,9 @@
     slot_at = lax.broadcasted_iota(I32, (CAPTOK, TOK), 0)
 
     def pack_for(to):
-        chosen = ((slot_at + to * CAPTOK) == tok[...]).astype(F32)
-        empty = jnp.sum(chosen, axis=1, keepdims=True) < 0.5
-        page_rows = nt(chosen.astype(BF16), rows[...])
+        chosen = ((slot_at + to * CAPTOK) == tok[...]).astype(F32).astype(BF16)
+        page_rows = nt(chosen, rows[...])
+        empty = page_rows[:, KVW + USED:KVW + USED + 1] < 0.5
         column = lax.broadcasted_iota(I32, (CAPTOK, KVX), 1)
         return jnp.where((column == KVW) & empty, 1.0, page_rows).astype(BF16)
 
@@ -402,7 +385,7 @@
     def pages_step(request, count, first, last):
         size, at = (last + 1 - first) * CAPTOK, columns(request, count)
         keys = arr[first:last + 1].reshape(size, KVX)
-        score = nt(keys, qbuf[pl.ds(c * NR + request, count)].reshape(count * QROWS, KVX))
+        score = nt(keys, qbuf[request:request + count].reshape(count * QROWS, KVX))
         old = ms[:, at]
         top = jnp.maximum(old, jnp.max(score, axis=0, keepdims=True))
         shrink = jnp.exp2((old - top) * log2_scale)
@@ -415,24 +398,18 @@
         at = columns(request, count)
         acc[:, at], ms[:, at], ls[:, at] = pages_step(request, count, first, last)
 
-    for pair in e_copies:
-        wait_pair(pair)
-    for r in range(NR):
-        add_other(r)
     ready((0, 1))
     turn_values(0, 1)
-    pages_of(0, 2, 0, 1)
+    pages_of(0, 4, 0, 1)
     swap((a_p[0], a_m[0]), (2, 3))
-    pages_of(2, 2, 0, 1)
     a_r0.wait_recv()
     go(a_f0)
     a_r1.wait_recv()
     go(a_f1)
     ready((2, 3))
     turn_values(2, 3)
-    pages_of(0, 2, 2, 3)
+    pages_of(0, 4, 2, 3)
     swap((a_p[1], a_m[1]), (4, 5))
-    pages_of(2, 2, 2, 3)
     ready((4, 5))
     turn_values(4, 5)
     swap((a_f0, a_f1), (6, 7))
@@ -590,13 +567,9 @@
             pltpu.VMEM((8, 2, HALF, KVX), BF16),
             pltpu.VMEM((1, TOK), I32),
             pltpu.VMEM((LATW, 8 * CAPTOK), BF16),
-            pltpu.VMEM((2 * NR, 4, 64, KVW), BF16),
-            pltpu.VMEM((2 * NR, QROWS, KVX), BF16),
-            pltpu.VMEM((2 * NR, KVW, CTXD), BF16),
-            pltpu.VMEM((NR, LATW, QROWS), I16),
-            pltpu.VMEM((NR, 3, 1, QROWS), F32),
-            pltpu.VMEM((NR, LATW, QROWS), I16),
-            pltpu.VMEM((NR, 3, 1, QROWS), F32),
+            pltpu.VMEM((NR, 4, 64, KVW), BF16),
+            pltpu.VMEM((NR, QROWS, KVX), BF16),
+            pltpu.VMEM((2, NR, KVW, CTXD), BF16),
             pltpu.VMEM((LATW, NR * QROWS), F32),
             pltpu.VMEM((1, NR * QROWS), F32),
             pltpu.VMEM((1, NR * QROWS), F32),

time: 68.9 us -> 68.6 us (level)
  no operation moved by 1% of the time
where the time goes in v9:
time: 68.6 us; the launch traced here: 68.5 us
  Pallas kernels  66.6 us (97%)
  local copies, waits for them, and re-layouts  1.87 us (3%)
    pallas_call x1, Pallas kernels, on_device(): pl.pallas_call(kernel, out_shape=jax.ShapeDtypeStruct((4, 2 * NR, 32, 64)...  66.6 us
    unnamed x1, local copies, waits for them, and re-layouts  1.87 us

profile of v9, /device:TPU:1, one launch (start us, length us, event | category | flops | bytes accessed | tf_op | source)
XLA Modules:
  0.0 68.5 jit_solution(15319070725739411906)
XLA Ops:
  0.0 66.6 %shard_map.100 = f32[4,8,32,64]{3,2,1,0:T(8,128)} custom-call(bf16[384,3584]{1,0:T(8,128)(2,1)} %hidden.1, bf16[144,3584]{1,0:T(8,128)(2,1)} %bitcast.7, f32[1,512]{1,0:T(1,128)} %bitcast.8, s32[1,24]{1,0:T(1,128)} %bitcast.9, s32[24]{0:T(128)} %request_in.1, bf16[4,8,64,576]{3,2,1,0:T(8,128)(2,1)} %queries.1, bf16[8,576,512]{2,1,0:T(8,128)(2,1)} %bitcast.6, ...), custom_call_target="tpu_custom_call" | custom-call | flops 7500000256 | bytes 12000000 | tf_op jit(solution)/shard_map/pallas_call | solution.py:544
  66.6 1.9 %copy.12 = f32[4,8,64,32]{2,3,1,0:T(8,128)} copy(f32[4,8,64,32]{2,3,1,0:T(8,128)} %bitcast.5) | data formatting | bytes 524288

commit v10 on v9

--- a/solution.py
+++ b/solution.py
@@ -45,7 +45,7 @@
     out_hbm,
     gain, owner, request, lengths, cosine, sine, out,
     hid, kvt, lat, mps, mpr, mss, msr, rows, packed, relay, arr, tok,
-    vt, qraw, qbuf, kbuf, acc, ms, ls, osend, ostat, ybuf, ystat, rsend, rstat, mbuf, mstat, fbuf, fstat,
+    vt, qraw, qbuf, kbuf, acc, ms, ls, osend, ostat, yfirst, yfstat, rsend, rstat, yrelay, yrstat, mbuf, mstat, fbuf, fstat,
     loc, send, recv,
 ):
     s, b, p = lax.axis_index("seq"), lax.axis_index("batch"), lax.axis_index("mp")
@@ -352,7 +352,7 @@
     a_r1 = link(packed.at[2, second], relay.at[1], dev_zm)
     a_f0 = link(relay.at[0], arr.at[6, c], dev_zp)
     a_f1 = link(relay.at[1], arr.at[7, c], dev_zm)
-    a_share = [link(arr.at[part, c], arr.at[part, c], dev_sib) for part in range(8)]
+    a_share = [link(arr.at[pl.ds(part, 2), c], arr.at[pl.ds(part, 2), c], dev_sib) for part in (0, 2, 4, 6)]
     packed[0] = pack_for(lax.rem(b + 1, 4))
     go(a_p[0])
     packed[1] = pack_for(lax.rem(b + 3, 4))
@@ -364,18 +364,13 @@
     go(a_m[1])
     own_pages = pack_for(b)
     arr[0, c] = own_pages[:HALF]
+    arr[1, c] = own_pages[HALF:]
     go(a_share[0])
-    arr[1, c] = own_pages[HALF:]
-    go(a_share[1])
-
-    def swap(copies, parts):
-        for copy, part in zip(copies, parts):
+
+    def swap(copies, group):
+        for copy in copies:
             copy.wait_recv()
-            go(a_share[part])
-
-    def ready(parts):
-        for part in parts:
-            a_share[part].wait_recv()
+        go(a_share[group])
 
     def turn_values(first, last):
         size = (last + 1 - first) * CAPTOK
@@ -398,23 +393,23 @@
         at = columns(request, count)
         acc[:, at], ms[:, at], ls[:, at] = pages_step(request, count, first, last)
 
-    ready((0, 1))
+    a_share[0].wait_recv()
     turn_values(0, 1)
     pages_of(0, 4, 0, 1)
-    swap((a_p[0], a_m[0]), (2, 3))
+    swap((a_p[0], a_m[0]), 1)
     a_r0.wait_recv()
     go(a_f0)
     a_r1.wait_recv()
     go(a_f1)
-    ready((2, 3))
+    a_share[1].wait_recv()
     turn_values(2, 3)
     pages_of(0, 4, 2, 3)
-    swap((a_p[1], a_m[1]), (4, 5))
-    ready((4, 5))
+    swap((a_p[1], a_m[1]), 2)
+    a_share[2].wait_recv()
     turn_values(4, 5)
-    swap((a_f0, a_f1), (6, 7))
+    swap((a_f0, a_f1), 3)
     pages_of(0, 2, 4, 5)
-    ready((6, 7))
+    a_share[3].wait_recv()
     turn_values(6, 7)
 
     def merge(parts):
@@ -434,94 +429,76 @@
         stat_ref[0] = top + jnp.log(scale) * log2_e
         stat_ref[1] = total / scale
 
-    yp, ym, yy = lax.rem(y + 1, 4), lax.rem(y + 3, 4), lax.rem(y + 2, 4)
-    first_y = used[0]
-
-    def y_pair(r, k):
-        pairs = (
-            (osend.at[r, yy, 0], ostat.at[r], 0, dev_yp),
-            (osend.at[r, yy, 1], ostat.at[r], 1, dev_ym),
-            (osend.at[r, yp, 1], ostat.at[r], 2, dev_yp),
-            (osend.at[r, ym, 0], ostat.at[r], 3, dev_ym),
-            (rsend.at[r, 0], rstat.at[r, 0], 4, dev_yp),
-            (rsend.at[r, 1], rstat.at[r, 1], 5, dev_ym),
-        )
-        data, stat, _, dev = pairs[k]
-        return (
-            link_at(first_y + 18 * r + 2 * k, data, ybuf.at[r, k], dev),
-            link_at(first_y + 18 * r + 2 * k + 1, stat, ystat.at[r, k], dev),
-        )
-
-    def last_pair(r, k):
-        half, core, dev = ((1 - xh, c, dev_x), (1 - xh, 1 - c, dev_x_sib), (xh, 1 - c, dev_sib))[k]
-        return (
-            link_at(first_y + 18 * r + 12 + 2 * k, mbuf.at[r, half, core], fbuf.at[r, k], dev),
-            link_at(first_y + 18 * r + 13 + 2 * k, mstat.at[r, half], fstat.at[r, k], dev),
-        )
-
-    def start_pair(pair):
-        pair[0].start()
-        pair[1].start()
-
-    def relay_sums(r, carry):
-        for k, to in ((0, yp), (1, ym)):
-            wait_pair(y_pair(r, k))
-            put(rsend.at[r, k], rstat.at[r, k], *merge([
-                (osend[r, to, k], ostat[r]), (ybuf[r, k], ystat[r, k]),
+    def both(data, stat, data_to, stat_to, dev):
+        return link(data, data_to, dev), link(stat, stat_to, dev)
+
+    first_copies, relay_copies, last_copies = [], [], []
+    for i in range(2):
+        first_copies.append([
+            both(osend.at[i, pl.ds(3 + 2 * k, 2)], ostat.at[i], yfirst.at[i, k], yfstat.at[i, k], dev)
+            for k, dev in enumerate((dev_yp, dev_ym))
+        ])
+        relay_copies.append([
+            both(rsend.at[i, k], rstat.at[i, k], yrelay.at[i, k], yrstat.at[i, k], dev)
+            for k, dev in enumerate((dev_yp, dev_ym))
+        ])
+        last_copies.append([
+            both(mbuf.at[i, half, core], mstat.at[i, half], fbuf.at[i, k], fstat.at[i, k], dev)
+            for k, (half, core, dev) in enumerate((
+                (1 - xh, c, dev_x), (1 - xh, 1 - c, dev_x_sib), (xh, 1 - c, dev_sib),
+            ))
+        ])
+
+    def relay_sums(i):
+        for k, (own, far) in enumerate(((2, 1), (7, 0))):
+            wait_pair(first_copies[i][k])
+            put(rsend.at[i, k], rstat.at[i, k], *merge([
+                (osend[i, own], ostat[i]), (yfirst[i, k, far], yfstat[i, k]),
             ]))
-            start_pair(y_pair(r, 4 + k))
-        return carry
-
-    for first_request, count, first in ((0, 1, 6), (1, 1, 6), (2, 2, 4)):
-        value, top, total = pages_step(first_request, count, first, 7)
-        coded, scale = code(value, 0)
-        coded, top, total = to_code(coded), top * log2_scale + jnp.log(scale) * log2_e, total / scale
-        for r in range(first_request, first_request + count):
-            at = columns(r - first_request)
-            osend[r] = coded[:, at].reshape(4, 2, 64, QROWS)
-            ostat[r, 0] = top[:, at]
-            ostat[r, 1] = total[:, at]
-            for k in range(4):
-                start_pair(y_pair(r, k))
-
-    def sums_over_y(r, carry):
-        for k in range(2, 6):
-            wait_pair(y_pair(r, k))
-        for h, (one, two) in enumerate(((3, 4), (2, 5))):
-            put(mbuf.at[r, h], mstat.at[r, h], *merge([
-                (osend[r, y, h], ostat[r]), (ybuf[r, one], ystat[r, one]), (ybuf[r, two], ystat[r, two]),
+            go_pair(relay_copies[i][k])
+
+    def sums_over_y(i):
+        for half in range(2):
+            wait_pair(relay_copies[i][half])
+            near = 1 - half
+            put(mbuf.at[i, half], mstat.at[i, half], *merge([
+                (osend[i, half], ostat[i]), (yfirst[i, near, near], yfstat[i, near]), (yrelay[i, half], yrstat[i, half]),
             ]))
         for k in (1, 0, 2):
-            start_pair(last_pair(r, k))
-        return carry
+            go_pair(last_copies[i][k])
 
     def out_copy(wanted):
         return pltpu.make_async_copy(out.at[:, wanted], out_hbm.at[:, wanted], loc.at[13 + wanted])
 
-    def last_sums(r, carry):
-        for k in range(3):
-            wait_pair(last_pair(r, k))
-        own, other = c * NR + r, (1 - c) * NR + r
-        for wanted, parts in (
-            (own, [(mbuf[r, xh, c], mstat[r, xh]), (fbuf[r, 0], fstat[r, 0])]),
-            (other, [(fbuf[r, 2], fstat[r, 2]), (fbuf[r, 1], fstat[r, 1])]),
+    def last_sums(i):
+        for pair in last_copies[i]:
+            wait_pair(pair)
+        for core, parts in (
+            (c, [(mbuf[i, xh, c], mstat[i, xh]), (fbuf[i, 0], fstat[i, 0])]),
+            (1 - c, [(fbuf[i, 2], fstat[i, 2]), (fbuf[i, 1], fstat[i, 1])]),
         ):
             value, _, total = merge(parts)
             value = value / total
-            for step in range(4):
-                out[step, wanted] = value[:, 64 * step:64 * step + 64]
-            out_copy(wanted).start()
-        return carry
-
-    def finish(r, carry):
-        for pair in [y_pair(r, k) for k in range(6)] + [last_pair(r, k) for k in range(3)]:
-            pair[0].wait_send()
-            pair[1].wait_send()
-        return carry
-
-    lax.fori_loop(0, NR, relay_sums, 0)
-    for stage in (sums_over_y, last_sums, finish):
-        lax.fori_loop(0, NR, stage, 0)
+            for j in range(2):
+                wanted = core * NR + 2 * i + j
+                for step in range(4):
+                    at = QROWS * j + 64 * step
+                    out[step, wanted] = value[:, at:at + 64]
+                out_copy(wanted).start()
+
+    for i, first in enumerate((6, 4)):
+        value, top, total = pages_step(2 * i, 2, first, 7)
+        coded, scale = code(value, 0)
+        blocks = to_code(coded).reshape(4, 2, 64, 2 * QROWS)
+        for chip in range(4):
+            osend[i, pl.ds(2 * lax.rem(chip - y + 4, 4), 2)] = blocks[chip]
+        ostat[i, 0] = top * log2_scale + jnp.log(scale) * log2_e
+        ostat[i, 1] = total / scale
+        for pair in first_copies[i]:
+            go_pair(pair)
+    for stage in (relay_sums, sums_over_y, last_sums):
+        for i in range(2):
+            stage(i)
     for wanted in range(2 * NR):
         out_copy(wanted).wait()
     for copy in started:
@@ -573,16 +550,18 @@
             pltpu.VMEM((LATW, NR * QROWS), F32),
             pltpu.VMEM((1, NR * QROWS), F32),
             pltpu.VMEM((1, NR * QROWS), F32),
-            pltpu.VMEM((NR, 4, 2, 64, QROWS), I16),
-            pltpu.VMEM((NR, 2, 1, QROWS), F32),
-            pltpu.VMEM((NR, 6, 64, QROWS), I16),
-            pltpu.VMEM((NR, 6, 2, 1, QROWS), F32),
-            pltpu.VMEM((NR, 2, 64, QROWS), I16),
-            pltpu.VMEM((NR, 2, 2, 1, QROWS), F32),
-            pltpu.VMEM((NR, 2, 2, 32, QROWS), I16),
-            pltpu.VMEM((NR, 2, 2, 1, QROWS), F32),
-            pltpu.VMEM((NR, 3, 32, QROWS), I16),
-            pltpu.VMEM((NR, 3, 2, 1, QROWS), F32),
+            pltpu.VMEM((2, 8, 64, 2 * QROWS), I16),
+            pltpu.VMEM((2, 2, 1, 2 * QROWS), F32),
+            pltpu.VMEM((2, 2, 2, 64, 2 * QROWS), I16),
+            pltpu.VMEM((2, 2, 2, 1, 2 * QROWS), F32),
+            pltpu.VMEM((2, 2, 64, 2 * QROWS), I16),
+            pltpu.VMEM((2, 2, 2, 1, 2 * QROWS), F32),
+            pltpu.VMEM((2, 2, 64, 2 * QROWS), I16),
+            pltpu.VMEM((2, 2, 2, 1, 2 * QROWS), F32),
+            pltpu.VMEM((2, 2, 2, 32, 2 * QROWS), I16),
+            pltpu.VMEM((2, 2, 2, 1, 2 * QROWS), F32),
+            pltpu.VMEM((2, 3, 32, 2 * QROWS), I16),
+            pltpu.VMEM((2, 3, 2, 1, 2 * QROWS), F32),
             pltpu.SemaphoreType.DMA((13 + 2 * NR,)),
             pltpu.SemaphoreType.DMA((LINKS,)),
             pltpu.SemaphoreType.DMA((LINKS,)),

time: 68.6 us -> 69.3 us (1.010)
  no operation moved by 1% of the time
where the time goes in v10:
time: 69.3 us; the launch traced here: 69.1 us
  Pallas kernels  67.2 us (97%)
  local copies, waits for them, and re-layouts  1.87 us (3%)
    pallas_call x1, Pallas kernels, on_device(): pl.pallas_call(kernel, out_shape=jax.ShapeDtypeStruct((4, 2 * NR, 32, 64)...  67.2 us
    unnamed x1, local copies, waits for them, and re-layouts  1.87 us

profile of v10, /device:TPU:1, one launch (start us, length us, event | category | flops | bytes accessed | tf_op | source)
XLA Modules:
  0.0 69.1 jit_solution(10616360923942326001)
XLA Ops:
  0.0 67.2 %shard_map.100 = f32[4,8,32,64]{3,2,1,0:T(8,128)} custom-call(bf16[384,3584]{1,0:T(8,128)(2,1)} %hidden.1, bf16[144,3584]{1,0:T(8,128)(2,1)} %bitcast.7, f32[1,512]{1,0:T(1,128)} %bitcast.8, s32[1,24]{1,0:T(1,128)} %bitcast.9, s32[24]{0:T(128)} %request_in.1, bf16[4,8,64,576]{3,2,1,0:T(8,128)(2,1)} %queries.1, bf16[8,576,512]{2,1,0:T(8,128)(2,1)} %bitcast.6, ...), custom_call_target="tpu_custom_call" | custom-call | flops 7500000256 | bytes 12000000 | tf_op jit(solution)/shard_map/pallas_call | solution.py:521
  67.2 1.9 %copy.12 = f32[4,8,64,32]{2,3,1,0:T(8,128)} copy(f32[4,8,64,32]{2,3,1,0:T(8,128)} %bitcast.5) | data formatting | bytes 524288

commit v11 on v9

--- a/solution.py
+++ b/solution.py
@@ -413,7 +413,7 @@
     ready((4, 5))
     turn_values(4, 5)
     swap((a_f0, a_f1), (6, 7))
-    pages_of(0, 2, 4, 5)
+    pages_of(0, 4, 4, 5)
     ready((6, 7))
     turn_values(6, 7)
 
@@ -472,17 +472,21 @@
             start_pair(y_pair(r, 4 + k))
         return carry
 
-    for first_request, count, first in ((0, 1, 6), (1, 1, 6), (2, 2, 4)):
-        value, top, total = pages_step(first_request, count, first, 7)
+    for r in range(NR):
+        value, top, total = pages_step(r, 1, 6, 7)
         coded, scale = code(value, 0)
-        coded, top, total = to_code(coded), top * log2_scale + jnp.log(scale) * log2_e, total / scale
-        for r in range(first_request, first_request + count):
-            at = columns(r - first_request)
-            osend[r] = coded[:, at].reshape(4, 2, 64, QROWS)
-            ostat[r, 0] = top[:, at]
-            ostat[r, 1] = total[:, at]
-            for k in range(4):
-                start_pair(y_pair(r, k))
+        osend[r] = to_code(coded).reshape(4, 2, 64, QROWS)
+        ostat[r, 0] = top * log2_scale + jnp.log(scale) * log2_e
+        ostat[r, 1] = total / scale
+        for k in (0, 1):
+            start_pair(y_pair(r, k))
+        if r >= 1:
+            for k in (2, 3):
+                start_pair(y_pair(r - 1, k))
+        if r >= 2:
+            lax.fori_loop(r - 2, r - 1, relay_sums, 0)
+    for k in (2, 3):
+        start_pair(y_pair(NR - 1, k))
 
     def sums_over_y(r, carry):
         for k in range(2, 6):
@@ -519,7 +523,7 @@
             pair[1].wait_send()
         return carry
 
-    lax.fori_loop(0, NR, relay_sums, 0)
+    lax.fori_loop(2, NR, relay_sums, 0)
     for stage in (sums_over_y, last_sums, finish):
         lax.fori_loop(0, NR, stage, 0)
     for wanted in range(2 * NR):

time: 68.6 us -> 69.1 us (level)
  no operation moved by 1% of the time
where the time goes in v11:
time: 69.1 us; the launch traced here: 68.9 us
  Pallas kernels  67.1 us (97%)
  local copies, waits for them, and re-layouts  1.87 us (3%)
    pallas_call x1, Pallas kernels, on_device(): pl.pallas_call(kernel, out_shape=jax.ShapeDtypeStruct((4, 2 * NR, 32, 64)...  67.1 us
    unnamed x1, local copies, waits for them, and re-layouts  1.87 us

profile of v11, /device:TPU:1, one launch (start us, length us, event | category | flops | bytes accessed | tf_op | source)
XLA Modules:
  0.0 68.9 jit_solution(14464076187469728608)
XLA Ops:
  0.0 67.1 %shard_map.100 = f32[4,8,32,64]{3,2,1,0:T(8,128)} custom-call(bf16[384,3584]{1,0:T(8,128)(2,1)} %hidden.1, bf16[144,3584]{1,0:T(8,128)(2,1)} %bitcast.7, f32[1,512]{1,0:T(1,128)} %bitcast.8, s32[1,24]{1,0:T(1,128)} %bitcast.9, s32[24]{0:T(128)} %request_in.1, bf16[4,8,64,576]{3,2,1,0:T(8,128)(2,1)} %queries.1, bf16[8,576,512]{2,1,0:T(8,128)(2,1)} %bitcast.6, ...), custom_call_target="tpu_custom_call" | custom-call | flops 7500000256 | bytes 12000000 | tf_op jit(solution)/shard_map/pallas_call | solution.py:548
  67.1 1.9 %copy.12 = f32[4,8,64,32]{2,3,1,0:T(8,128)} copy(f32[4,8,64,32]{2,3,1,0:T(8,128)} %bitcast.5) | data formatting | bytes 524288

commit v12 on v9

--- a/solution.py
+++ b/solution.py
@@ -42,8 +42,8 @@
 
 def kernel(
     hidden, kv_down, gain_in, owner_in, request_in, queries, cache, lengths_in, cosine_in, sine_in,
-    out_hbm,
-    gain, owner, request, lengths, cosine, sine, out,
+    out_hbm, inverse_hbm,
+    gain, owner, request, lengths, cosine, sine, out, inverses,
     hid, kvt, lat, mps, mpr, mss, msr, rows, packed, relay, arr, tok,
     vt, qraw, qbuf, kbuf, acc, ms, ls, osend, ostat, ybuf, ystat, rsend, rstat, mbuf, mstat, fbuf, fstat,
     loc, send, recv,
@@ -507,9 +507,10 @@
             (other, [(fbuf[r, 2], fstat[r, 2]), (fbuf[r, 1], fstat[r, 1])]),
         ):
             value, _, total = merge(parts)
-            value = value / total
+            total = 1.0 / total
             for step in range(4):
                 out[step, wanted] = value[:, 64 * step:64 * step + 64]
+                inverses[step, wanted] = total[:, 64 * step:64 * step + 64]
             out_copy(wanted).start()
         return carry
 
@@ -520,10 +521,14 @@
         return carry
 
     lax.fori_loop(0, NR, relay_sums, 0)
-    for stage in (sums_over_y, last_sums, finish):
+    for stage in (sums_over_y, last_sums):
         lax.fori_loop(0, NR, stage, 0)
+    inverse_copy = pltpu.make_async_copy(inverses, inverse_hbm, loc.at[13 + 2 * NR])
+    inverse_copy.start()
     for wanted in range(2 * NR):
         out_copy(wanted).wait()
+    inverse_copy.wait()
+    lax.fori_loop(0, NR, finish, 0)
     for copy in started:
         copy.wait_send()
 
@@ -541,11 +546,13 @@
 def on_device(hidden, kv_down, kv_gain, page_owner, page_request, queries, cache, lengths):
     cosine, sine = tables()
     anywhere = pl.BlockSpec(memory_space=pl.ANY)
-    sums = pl.pallas_call(
+    sums, inverse = pl.pallas_call(
         kernel,
-        out_shape=jax.ShapeDtypeStruct((4, 2 * NR, 32, 64), F32),
+        out_shape=(
+            jax.ShapeDtypeStruct((4, 2 * NR, 32, 64), F32), jax.ShapeDtypeStruct((4, 2 * NR, 1, 64), F32),
+        ),
         in_specs=[anywhere] * 10,
-        out_specs=anywhere,
+        out_specs=(anywhere, anywhere),
         scratch_shapes=[
             pltpu.VMEM((1, LATW), F32),
             pltpu.SMEM((1, PAGES), I32),
@@ -554,6 +561,7 @@
             pltpu.VMEM((ROPEW // 2, TOK), F32),
             pltpu.VMEM((ROPEW // 2, TOK), F32),
             pltpu.VMEM((4, 2 * NR, 32, 64), F32),
+            pltpu.VMEM((4, 2 * NR, 1, 64), F32),
             pltpu.VMEM((TOK, HALF_D), BF16),
             pltpu.VMEM((4, BLK, HALF_D), BF16),
             pltpu.VMEM((4, BLK, TOK), F32),
@@ -583,7 +591,7 @@
             pltpu.VMEM((NR, 2, 2, 1, QROWS), F32),
             pltpu.VMEM((NR, 3, 32, QROWS), I16),
             pltpu.VMEM((NR, 3, 2, 1, QROWS), F32),
-            pltpu.SemaphoreType.DMA((13 + 2 * NR,)),
+            pltpu.SemaphoreType.DMA((14 + 2 * NR,)),
             pltpu.SemaphoreType.DMA((LINKS,)),
             pltpu.SemaphoreType.DMA((LINKS,)),
         ],
@@ -595,7 +603,7 @@
         hidden, kv_down.T, kv_gain.reshape(1, LATW), page_owner.T, page_request, queries, cache.transpose(0, 2, 1), lengths,
         jnp.asarray(cosine), jnp.asarray(sine),
     )
-    return sums.transpose(0, 1, 3, 2)
+    return (sums * inverse).transpose(0, 1, 3, 2)
 
 
 def solution(mesh):

time: 68.6 us -> 68.7 us (level)
  other arithmetic: 0 us -> 1.9 us
  local copies, waits for them, and re-layouts: 1.87 us -> 0 us
    transpose x0 -> x1, other arithmetic: none -> 1.9 us  [on_device(): return (sums * inverse).transpose(0, 1, 3, 2)]
    unnamed x1 -> x0, local copies, waits for them, and re-layouts: 1.87 us -> none
where the time goes in v12:
time: 68.7 us; the launch traced here: 68.6 us
  Pallas kernels  66.7 us (97%)
  other arithmetic  1.9 us (3%)
    pallas_call x1, Pallas kernels, on_device(): pl.pallas_call(kernel, out_shape=(jax.ShapeDtypeStruct((4, 2 * NR, 32, 64...  66.7 us
    transpose x1, other arithmetic, on_device(): return (sums * inverse).transpose(0, 1, 3, 2)  1.9 us

profile of v12, /device:TPU:1, one launch (start us, length us, event | category | flops | bytes accessed | tf_op | source)
XLA Modules:
  0.0 68.6 jit_solution(16610063084177396873)
XLA Ops:
  0.0 66.7 %shard_map.100 = (f32[4,8,32,64]{3,2,1,0:T(8,128)}, f32[4,8,1,64]{3,2,1,0:T(1,128)}) custom-call(bf16[384,3584]{1,0:T(8,128)(2,1)} %hidden.1, bf16[144,3584]{1,0:T(8,128)(2,1)} %bitcast.9, f32[1,512]{1,0:T(1,128)} %bitcast.10, s32[1,24]{1,0:T(1,128)} %bitcast.11, s32[24]{0:T(128)} %request_in.1, bf16[4,8,64,576]{3,2,1,0:T(8,128)(2,1)} %queries.1, ...), custom_call_target="tpu_custom_call" | custom-call | flops 7500000256 | bytes 12000000 | tf_op jit(solution)/shard_map/pallas_call | solution.py:549
  66.7 1.9 %multiply_bitcast_fusion = f32[4,8,64,32]{2,3,1,0:T(8,128)} fusion(f32[4,8,32,64]{3,2,1,0:T(8,128)} %get-tuple-element.7, f32[4,8,64]{2,1,0:T(8,128)} %bitcast.7), kind=kLoop, calls=%fused_computation | loop fusion | flops 65536 | bytes 532480 | tf_op jit(solution)/shard_map/transpose | solution.py:606

commit v13 on v9

--- a/solution.py
+++ b/solution.py
@@ -408,7 +408,7 @@
     go(a_f1)
     ready((2, 3))
     turn_values(2, 3)
-    pages_of(0, 4, 2, 3)
+    pages_of(0, 2, 2, 3)
     swap((a_p[1], a_m[1]), (4, 5))
     ready((4, 5))
     turn_values(4, 5)
@@ -472,7 +472,7 @@
             start_pair(y_pair(r, 4 + k))
         return carry
 
-    for first_request, count, first in ((0, 1, 6), (1, 1, 6), (2, 2, 4)):
+    for first_request, count, first in ((0, 1, 6), (1, 1, 6), (2, 2, 2)):
         value, top, total = pages_step(first_request, count, first, 7)
         coded, scale = code(value, 0)
         coded, top, total = to_code(coded), top * log2_scale + jnp.log(scale) * log2_e, total / scale

time: 68.6 us -> 69 us (level)
  no operation moved by 1% of the time
where the time goes in v13:
time: 69 us; the launch traced here: 68.8 us
  Pallas kernels  66.9 us (97%)
  local copies, waits for them, and re-layouts  1.87 us (3%)
    pallas_call x1, Pallas kernels, on_device(): pl.pallas_call(kernel, out_shape=jax.ShapeDtypeStruct((4, 2 * NR, 32, 64)...  66.9 us
    unnamed x1, local copies, waits for them, and re-layouts  1.87 us

profile of v13, /device:TPU:1, one launch (start us, length us, event | category | flops | bytes accessed | tf_op | source)
XLA Modules:
  0.0 68.8 jit_solution(689629788881240116)
XLA Ops:
  0.0 66.9 %shard_map.100 = f32[4,8,32,64]{3,2,1,0:T(8,128)} custom-call(bf16[384,3584]{1,0:T(8,128)(2,1)} %hidden.1, bf16[144,3584]{1,0:T(8,128)(2,1)} %bitcast.7, f32[1,512]{1,0:T(1,128)} %bitcast.8, s32[1,24]{1,0:T(1,128)} %bitcast.9, s32[24]{0:T(128)} %request_in.1, bf16[4,8,64,576]{3,2,1,0:T(8,128)(2,1)} %queries.1, bf16[8,576,512]{2,1,0:T(8,128)(2,1)} %bitcast.6, ...), custom_call_target="tpu_custom_call" | custom-call | flops 7500000256 | bytes 12000000 | tf_op jit(solution)/shard_map/pallas_call | solution.py:544
  66.9 1.9 %copy.12 = f32[4,8,64,32]{2,3,1,0:T(8,128)} copy(f32[4,8,64,32]{2,3,1,0:T(8,128)} %bitcast.5) | data formatting | bytes 524288

commit v14 on v9

--- a/solution.py
+++ b/solution.py
@@ -382,7 +382,7 @@
         values = arr[first:last + 1].reshape(size, KVX)[:, :LATW]
         vt[:, first * CAPTOK:first * CAPTOK + size] = jnp.transpose(values)
 
-    def pages_step(request, count, first, last):
+    def pages_step(request, count, first, last, between=lambda: None):
         size, at = (last + 1 - first) * CAPTOK, columns(request, count)
         keys = arr[first:last + 1].reshape(size, KVX)
         score = nt(keys, qbuf[request:request + count].reshape(count * QROWS, KVX))
@@ -391,6 +391,7 @@
         shrink = jnp.exp2((old - top) * log2_scale)
         w = weigh(score, top)
         total = ls[:, at] * shrink + jnp.sum(w, axis=0, keepdims=True)
+        between()
         value = acc[:, at] * shrink + nn(vt[:, first * CAPTOK:first * CAPTOK + size], w.astype(BF16))
         return value, top, total
 
@@ -473,7 +474,8 @@
         return carry
 
     for first_request, count, first in ((0, 1, 6), (1, 1, 6), (2, 2, 4)):
-        value, top, total = pages_step(first_request, count, first, 7)
+        relay = (lambda: lax.fori_loop(0, 2, relay_sums, 0)) if first_request == 2 else (lambda: None)
+        value, top, total = pages_step(first_request, count, first, 7, relay)
         coded, scale = code(value, 0)
         coded, top, total = to_code(coded), top * log2_scale + jnp.log(scale) * log2_e, total / scale
         for r in range(first_request, first_request + count):
@@ -519,7 +521,7 @@
             pair[1].wait_send()
         return carry
 
-    lax.fori_loop(0, NR, relay_sums, 0)
+    lax.fori_loop(2, NR, relay_sums, 0)
     for stage in (sums_over_y, last_sums, finish):
         lax.fori_loop(0, NR, stage, 0)
     for wanted in range(2 * NR):

time: 68.6 us -> 70.4 us (1.026)
  Pallas kernels: 66.6 us -> 68.3 us
    pallas_call x1, Pallas kernels: 66.6 us -> 68.3 us  [on_device(): pl.pallas_call(kernel, out_shape=jax.ShapeDtypeStruct((4, 2 * NR, 32, 64)...]
where the time goes in v14:
time: 70.4 us; the launch traced here: 70.2 us
  Pallas kernels  68.3 us (97%)
  local copies, waits for them, and re-layouts  1.87 us (3%)
    pallas_call x1, Pallas kernels, on_device(): pl.pallas_call(kernel, out_shape=jax.ShapeDtypeStruct((4, 2 * NR, 32, 64)...  68.3 us
    unnamed x1, local copies, waits for them, and re-layouts  1.87 us

profile of v14, /device:TPU:1, one launch (start us, length us, event | category | flops | bytes accessed | tf_op | source)
XLA Modules:
  0.0 70.2 jit_solution(5619521835595512644)
XLA Ops:
  0.0 68.3 %shard_map.100 = f32[4,8,32,64]{3,2,1,0:T(8,128)} custom-call(bf16[384,3584]{1,0:T(8,128)(2,1)} %hidden.1, bf16[144,3584]{1,0:T(8,128)(2,1)} %bitcast.7, f32[1,512]{1,0:T(1,128)} %bitcast.8, s32[1,24]{1,0:T(1,128)} %bitcast.9, s32[24]{0:T(128)} %request_in.1, bf16[4,8,64,576]{3,2,1,0:T(8,128)(2,1)} %queries.1, bf16[8,576,512]{2,1,0:T(8,128)(2,1)} %bitcast.6, ...), custom_call_target="tpu_custom_call" | custom-call | flops 7500000256 | bytes 12000000 | tf_op jit(solution)/shard_map/pallas_call | solution.py:546
  68.4 1.9 %copy.12 = f32[4,8,64,32]{2,3,1,0:T(8,128)} copy(f32[4,8,64,32]{2,3,1,0:T(8,128)} %bitcast.5) | data formatting | bytes 524288

commit v15 on v9

--- a/solution.py
+++ b/solution.py
@@ -472,7 +472,7 @@
             start_pair(y_pair(r, 4 + k))
         return carry
 
-    for first_request, count, first in ((0, 1, 6), (1, 1, 6), (2, 2, 4)):
+    for first_request, count, first in ((0, 2, 6), (2, 2, 4)):
         value, top, total = pages_step(first_request, count, first, 7)
         coded, scale = code(value, 0)
         coded, top, total = to_code(coded), top * log2_scale + jnp.log(scale) * log2_e, total / scale

time: 68.6 us -> 68.6 us (level)
  no operation moved by 1% of the time
where the time goes in v15:
time: 68.6 us; the launch traced here: 68.4 us
  Pallas kernels  66.6 us (97%)
  local copies, waits for them, and re-layouts  1.87 us (3%)
    pallas_call x1, Pallas kernels, on_device(): pl.pallas_call(kernel, out_shape=jax.ShapeDtypeStruct((4, 2 * NR, 32, 64)...  66.6 us
    unnamed x1, local copies, waits for them, and re-layouts  1.87 us

profile of v15, /device:TPU:1, one launch (start us, length us, event | category | flops | bytes accessed | tf_op | source)
XLA Modules:
  0.0 68.4 jit_solution(15999820366139974532)
XLA Ops:
  0.0 66.6 %shard_map.100 = f32[4,8,32,64]{3,2,1,0:T(8,128)} custom-call(bf16[384,3584]{1,0:T(8,128)(2,1)} %hidden.1, bf16[144,3584]{1,0:T(8,128)(2,1)} %bitcast.7, f32[1,512]{1,0:T(1,128)} %bitcast.8, s32[1,24]{1,0:T(1,128)} %bitcast.9, s32[24]{0:T(128)} %request_in.1, bf16[4,8,64,576]{3,2,1,0:T(8,128)(2,1)} %queries.1, bf16[8,576,512]{2,1,0:T(8,128)(2,1)} %bitcast.6, ...), custom_call_target="tpu_custom_call" | custom-call | flops 7500000256 | bytes 12000000 | tf_op jit(solution)/shard_map/pallas_call | solution.py:544
  66.6 1.9 %copy.12 = f32[4,8,64,32]{2,3,1,0:T(8,128)} copy(f32[4,8,64,32]{2,3,1,0:T(8,128)} %bitcast.5) | data formatting | bytes 524288

commit v16 on v15

--- a/solution.py
+++ b/solution.py
@@ -413,7 +413,7 @@
     ready((4, 5))
     turn_values(4, 5)
     swap((a_f0, a_f1), (6, 7))
-    pages_of(0, 2, 4, 5)
+    pages_of(0, 4, 4, 5)
     ready((6, 7))
     turn_values(6, 7)
 
@@ -472,7 +472,7 @@
             start_pair(y_pair(r, 4 + k))
         return carry
 
-    for first_request, count, first in ((0, 2, 6), (2, 2, 4)):
+    for first_request, count, first in ((0, 2, 6), (2, 2, 6)):
         value, top, total = pages_step(first_request, count, first, 7)
         coded, scale = code(value, 0)
         coded, top, total = to_code(coded), top * log2_scale + jnp.log(scale) * log2_e, total / scale

time: 68.6 us -> 68.9 us (level)
  no operation moved by 1% of the time
where the time goes in v16:
time: 68.9 us; the launch traced here: 68.8 us
  Pallas kernels  66.9 us (97%)
  local copies, waits for them, and re-layouts  1.87 us (3%)
    pallas_call x1, Pallas kernels, on_device(): pl.pallas_call(kernel, out_shape=jax.ShapeDtypeStruct((4, 2 * NR, 32, 64)...  66.9 us
    unnamed x1, local copies, waits for them, and re-layouts  1.87 us

profile of v16, /device:TPU:1, one launch (start us, length us, event | category | flops | bytes accessed | tf_op | source)
XLA Modules:
  0.0 68.8 jit_solution(10475512504012941480)
XLA Ops:
  0.0 66.9 %shard_map.100 = f32[4,8,32,64]{3,2,1,0:T(8,128)} custom-call(bf16[384,3584]{1,0:T(8,128)(2,1)} %hidden.1, bf16[144,3584]{1,0:T(8,128)(2,1)} %bitcast.7, f32[1,512]{1,0:T(1,128)} %bitcast.8, s32[1,24]{1,0:T(1,128)} %bitcast.9, s32[24]{0:T(128)} %request_in.1, bf16[4,8,64,576]{3,2,1,0:T(8,128)(2,1)} %queries.1, bf16[8,576,512]{2,1,0:T(8,128)(2,1)} %bitcast.6, ...), custom_call_target="tpu_custom_call" | custom-call | flops 7500000256 | bytes 12000000 | tf_op jit(solution)/shard_map/pallas_call | solution.py:544
  66.9 1.9 %copy.12 = f32[4,8,64,32]{2,3,1,0:T(8,128)} copy(f32[4,8,64,32]{2,3,1,0:T(8,128)} %bitcast.5) | data formatting | bytes 524288
